TPU v7x, 512 devices: a whole 4x8x8 slice. The times are simulated.
512 devices in a mesh: depth: 8 (over x, z_lo), row: 8 (over y), col: 8 (over z_hi, core).
Axes of the slice: x: 4, y: 8, z: 8 (z_hi: 4, z_lo: 2; z = z_hi * 2 + z_lo), core: 2. Of those that a mesh axis runs over, the one named last changes fastest.
Arguments:
- half_slabs: bfloat16 [2, 4000, 8192], P(None, 'depth', ('row', 'col')), may hold values from -6 to 6
- virtuals: bfloat16 [4000, 3456], P('col', 'depth'), may hold values from -0.015625 to 0.015625
- occupied_energy: float32 [2], replicated, may hold values from -2 to -0.3
- virtual_energy: float32 [3456], P('depth'), may hold values from 0.1 to 3
- frequency: float32 [1], replicated, may hold values from 0.2 to 2
Outputs:
- gram_block: float32 [8192, 8192], P('row', 'col')
All inputs are finite; a program needn't handle non-finite values.
Results may differ from a plain program's by a relative error of at most 0.003.
Values may be sent and summed in bfloat16 or wider, within the bound.
A program may use at most 64 MiB of HBM per device.

v0:
```python
import jax
import jax.numpy as jnp
from jax import lax
from jax.sharding import PartitionSpec as P


def broadcast(block, axis, source):
    block = jnp.where(lax.axis_index(axis) == source, block, jnp.zeros_like(block))
    return lax.psum(block, axis)


def on_device(half_slabs, virtuals, occupied_energy, virtual_energy, frequency):
    coefficients = lax.all_gather(virtuals, "col", axis=0, tiled=True)
    orbitals = half_slabs.shape[0]
    local_vir = coefficients.shape[1]
    piece_cols = half_slabs.shape[2]
    coupling = jnp.einsum(
        "inp,na->iap",
        lax.all_gather(half_slabs, "depth", axis=1, tiled=True),
        coefficients,
        preferred_element_type=jnp.float32,
    ).astype(jnp.bfloat16)
    row_panel = lax.all_gather(coupling, "col", axis=2, tiled=True)
    row_count = lax.axis_size("row")
    col_count = lax.axis_size("col")
    grid_ratio = col_count // row_count
    block_width = row_count * piece_cols
    source_row = lax.axis_index("col") // grid_ratio
    shared_panel = broadcast(row_panel, "row", source_row)
    excitation = virtual_energy[None, :] - occupied_energy[:, None]
    weight = 4.0 * excitation / (excitation * excitation + frequency[0] * frequency[0])
    weighted = (weight[:, :, None] * row_panel.astype(jnp.float32)).astype(jnp.bfloat16)
    weighted_rows = weighted.reshape(orbitals * local_vir, row_panel.shape[2])
    plain_rows = shared_panel.reshape(orbitals * local_vir, block_width)
    partial_gram = lax.dot_general(
        weighted_rows, plain_rows, (((0,), (0,)), ((), ())), preferred_element_type=jnp.float32
    )
    gram_block = lax.psum(partial_gram, "depth")
    return gram_block


def solution(mesh):
    placed = (P(None, "depth", ("row", "col")), P("col", "depth"), P(), P("depth"), P())
    return jax.shard_map(
        on_device, mesh=mesh, in_specs=placed, out_specs=P("row", "col"), check_vma=False
    )
```

profile of v0, /device:TPU:1, one launch (start us, length us, event | category | flops | bytes accessed | tf_op | source)
XLA Modules:
  0.0 462.9 jit_solution(6793472588867779673)
XLA Ops:
  6.5 0.0 all-gather.9.cloned.1.call-start
  6.5 0.7 all-gather.9.cloned.1.call-update
  7.3 0.0 all-gather.5.cloned.1.call-start
  7.3 0.7 all-gather.5.cloned.1.call-update
  8.0 0.0 all-gather.7.cloned.1.call-start
  8.1 58.3 %all-gather.9.cloned.1.call-done = bf16[8,500,432]{1,2,0:T(8,128)(2,1)} async-done(((bf16[1,500,432]{1,2,0:T(8,128)(2,1)}), bf16[8,500,432]{1,2,0:T(8,128)(2,1)}) %all-gather.9.cloned.1.call-update) | async-done | bytes 3456016 | tf_op jit(solution)/shard_map/all_gather | solution.py:13
  66.4 4.0 copy.8
  70.3 8.0 %reshape.36 = bf16[4000,432,1]{0,1,2:T(8,128)(2,1)} reshape(bf16[8,500,432]{1,0,2:T(8,128)(2,1)S(1)} %copy.8) | data formatting | bytes 6912000
  78.3 44.0 %all-gather.5.cloned.1.call-done = bf16[2,4000,128]{2,0,1:T(2,128)(2,1)} async-done(((bf16[2,500,128]{2,0,1:T(2,128)(2,1)}), bf16[2,4000,128]{2,0,1:T(2,128)(2,1)}) %all-gather.5.cloned.1.call-update) | async-done | bytes 2048016 | tf_op jit(solution)/shard_map/all_gather | solution.py:19
  122.4 4.4 fusion.6
  126.8 0.0 all-gather.7.cloned.1.call-update
  126.8 0.0 all-reduce.3.cloned.1.call-start
  126.9 0.0 copy-start.1
  126.9 0.0 copy-start.2
  126.9 40.9 %all-gather.7.cloned.1.call-done = bf16[2,432,1024]{2,1,0:T(8,128)(2,1)} async-done(((bf16[2,432,128]{2,1,0:T(8,128)(2,1)}), bf16[2,432,1024]{2,1,0:T(8,128)(2,1)}) %all-gather.7.cloned.1.call-update) | async-done | bytes 1769488 | tf_op jit(solution)/shard_map/all_gather | solution.py:23
  167.8 0.0 copy-start
  167.8 1.3 broadcast_select_fusion
  169.1 0.0 all-reduce.3.cloned.1.call-update
  169.1 0.0 all-reduce.5.cloned.1.call-start
  169.8 0.0 copy-done.1
  169.8 0.0 copy-done.2
  169.8 0.1 fusion.9
  169.9 78.8 %all-reduce.3.cloned.1.call-done = bf16[2,432,1024]{2,1,0:T(8,128)(2,1)} async-done(((bf16[2,432,1024]{2,1,0:T(8,128)(2,1)}), bf16[2,432,1024]{2,1,0:T(8,128)(2,1)}) %all-reduce.3.cloned.1.call-update) | async-done | bytes 1769488 | tf_op jit(solution)/shard_map/psum | solution.py:9
  248.7 0.0 copy-done
  248.7 6.0 %convolution_bitcast_fusion = f32[1024,1024]{1,0:T(8,128)} fusion(bf16[2,432,1024]{2,1,0:T(8,128)(2,1)} %all-reduce.3.cloned.1.call-done, bf16[2,432,1024]{2,1,0:T(8,128)(2,1)S(1)} %copy-done, f32[2,432]{1,0:T(2,128)S(1)} %fusion.9), kind=kOutput, calls=%fused_computation.1 | convolution fusion | flops 1814593536 | bytes 7736704 | tf_op jit(solution)/shard_map/dot_general | solution.py:35
  254.6 0.0 all-reduce.5.cloned.1.call-update
  254.7 196.9 %all-reduce.5.cloned.1.call-done = f32[1024,1024]{1,0:T(8,128)} async-done(((f32[1024,1024]{1,0:T(8,128)}), f32[1024,1024]{1,0:T(8,128)}) %all-reduce.5.cloned.1.call-update) | async-done | bytes 4194320 | tf_op jit(solution)/shard_map/psum | solution.py:38
  451.5 4.8 %copy.19 = f32[1024,1024]{1,0:T(8,128)} copy(f32[1024,1024]{1,0:T(8,128)} %all-reduce.5.cloned.1.call-done) | data formatting | bytes 8388608
Async XLA Ops:
  6.5 59.8 %all-gather.9.cloned.1.call-start = ((), (), s32[]{:S(2)}) async-start(), calls=%async_computation.4 | async-start | bytes 3981312 | tf_op jit(solution)/shard_map/all_gather | solution.py:13
  7.3 115.1 %all-gather.5.cloned.1.call-start = ((), (), s32[]{:S(2)}) async-start(), calls=%async_computation | async-start | bytes 2304000 | tf_op jit(solution)/shard_map/all_gather | solution.py:19
  8.0 159.8 %all-gather.7.cloned.1.call-start = ((), (), s32[]{:S(2)}) async-start(), calls=%async_computation.1 | async-start | bytes 1990656 | tf_op jit(solution)/shard_map/all_gather | solution.py:23
  126.8 121.9 %all-reduce.3.cloned.1.call-start = ((), (), s32[]{:S(2)}) async-start(), calls=%async_computation.2 | async-start | bytes 3538944 | tf_op jit(solution)/shard_map/psum | solution.py:9
  126.9 43.0 %copy-start.1 = (f32[432]{0:T(512)S(1)}, f32[432]{0:T(512)}, u32[]{:S(2)}) copy-start(f32[432]{0:T(512)} %param.8) | copy-start | bytes 5188
  126.9 42.9 %copy-start.2 = (f32[2]{0:T(128)S(1)}, f32[2]{0:T(128)}, u32[]{:S(2)}) copy-start(f32[2]{0:T(128)} %param.7) | copy-start | bytes 28
  167.8 80.9 %copy-start = (bf16[2,432,1024]{2,1,0:T(8,128)(2,1)S(1)}, bf16[2,432,1024]{2,1,0:T(8,128)(2,1)}, u32[]{:S(2)}) copy-start(bf16[2,432,1024]{2,1,0:T(8,128)(2,1)} %all-gather.7.cloned.1.call-done) | copy-start | bytes 5308420
  169.1 282.4 %all-reduce.5.cloned.1.call-start = ((), (), s32[]{:S(2)}) async-start(), calls=%async_computation.3 | async-start | bytes 8388608 | tf_op jit(solution)/shard_map/psum | solution.py:38
Sparse Core Ops, SparseCore 0:
  9.5 56.8 all-gather.8
  68.5 53.8 all-gather.4
  126.9 40.7 all-gather.6
  170.0 78.6 all-reduce.2
  254.8 196.7 all-reduce.4
where the time goes:
time: 463 us
  waiting for transfers between devices  420 us (91%)
  local copies, waits for them, and re-layouts  16.8 us (4%)
  between operations  13.8 us (3%)
  matrix products  10.4 us (2%)
    psum x1, waiting for transfers between devices, on_device(): gram_block = lax.psum(partial_gram, 'depth')  197 us
    psum x1, waiting for transfers between devices, broadcast(): return lax.psum(block, axis)  78.8 us
    all_gather x1, waiting for transfers between devices, on_device(): coefficients = lax.all_gather(virtuals, 'col', axis=0, tiled=True)  58.3 us
    all_gather x1, waiting for transfers between devices, on_device(): lax.all_gather(half_slabs, 'depth', axis=1, tiled=True)  44 us
    all_gather x1, waiting for transfers between devices, on_device(): row_panel = lax.all_gather(coupling, 'col', axis=2, tiled=True)  40.9 us
    unnamed x8, local copies, waits for them, and re-layouts  12.8 us
  transfers between devices with their start and end apart: 5, of which 5 were waited for; matrix products, arithmetic and copies ran while one was open for 3% of the time, Pallas kernels for 0%

commit v1 on v0

v1 whole, which is shorter than its diff:
```python
import jax
import jax.numpy as jnp
from jax import lax
from jax.experimental import pallas as pl
from jax.experimental.pallas import tpu as pltpu
from jax.sharding import PartitionSpec as P

MESH = pl.DeviceIdType.MESH
BF = jnp.bfloat16
F32 = jnp.float32
RING = 8
LANES = 128


class Links:
    def __init__(self, send_sems, recv_sems):
        self.send_sems, self.recv_sems, self.copies = send_sems, recv_sems, []

    def plan(self, src, dst, **target):
        at = len(self.copies)
        copy = pltpu.make_async_remote_copy(
            src_ref=src,
            dst_ref=dst,
            send_sem=self.send_sems.at[at],
            recv_sem=self.recv_sems.at[at],
            device_id=target,
            device_id_type=MESH,
        )
        self.copies.append(copy)
        return copy

    def send(self, src, dst, **target):
        copy = self.plan(src, dst, **target)
        copy.start()
        return copy

    def finish(self):
        for copy in self.copies:
            copy.wait_send()


def around(me):
    up, down, far = lax.rem(me + 2, RING), lax.rem(me + 6, RING), lax.rem(me + 4, RING)
    return up, down, far, me + 1 - 2 * lax.rem(me, 2)


def other(at):
    return at + 1 - 2 * lax.rem(at, 2)


def gather_kernel(
    slabs_ref, virt_ref, vir_energy_ref, occ_ref, freq_ref, out_ref,
    slab_in, virt_in, energy_in, occ_in, freq_in, vpad, vq, hs, acc, rp, qp, wrow, wcol, wl,
    a_raw, a_land, a_keep, a_own, a_sib, a_last,
    b_terms, b_raw, b_land, b_keep, b_own, b_give, b_take, red,
    local_sems, send_sems, recv_sems,
):
    d, r, c = lax.axis_index("depth"), lax.axis_index("row"), lax.axis_index("col")
    d_up, d_down, d_far, d_sib = around(d)
    c_up, c_down, c_far, c_sib = around(c)
    r_up, r_down = lax.rem(r + 1, RING), lax.rem(r + 7, RING)
    links = Links(send_sems, recv_sems)
    send = links.send

    loads = [
        pltpu.make_async_copy(src, dst, local_sems.at[at])
        for at, (src, dst) in enumerate(
            (
                (virt_ref, virt_in), (slabs_ref, slab_in), (vir_energy_ref, energy_in),
                (occ_ref, occ_in), (freq_ref, freq_in),
            )
        )
    ]
    for load in loads:
        load.start()
    barrier = pltpu.get_barrier_semaphore()
    partners = [{"depth": d_up}, {"depth": d_down}, {"depth": d_sib}, {"row": r_up}, {"row": r_down}]
    partners += [{"col": lax.rem(c + step, RING)} for step in range(1, RING)]
    for partner in partners:
        pl.semaphore_signal(barrier, inc=1, device_id=partner, device_id_type=MESH)

    nbas, nvir = virt_ref.shape
    vpad[...] = jnp.zeros_like(vpad)
    for load in loads:
        load.wait()
    vpad[0:nbas, 0:nvir] = virt_in[...]
    for quarter in range(4):
        block = vpad[128 * quarter : 128 * quarter + 128, :]
        vq[c, quarter] = block.T[0:nvir, :]
    for orbital in range(2):
        hs[d, orbital, 496:512, :] = jnp.zeros((16, LANES), BF)
        hs[d, orbital, 0:nbas, :] = slab_in[orbital]

    pl.semaphore_wait(barrier, len(partners))

    j = lax.rem(r, 4)
    j_up, j_down = lax.rem(j + 1, 4), lax.rem(j + 3, 4)
    spans = (pl.ds(0, 208), pl.ds(208, 224))

    def slab(n, orbital, **target):
        return send(hs.at[n, orbital], hs.at[n, orbital], **target)

    def virt(n, quarter, half, **target):
        piece = vq.at[n, quarter, spans[half]]
        return send(piece, piece, **target)

    def virt_rows(n, half):
        return virt(n, j, half, row=r_up), virt(n, j, half, row=r_down)

    pair = {1: slab(d, 1, depth=d_sib), 0: slab(d, 0, depth=d_sib)}
    z_up = {1: virt(c, j, 1, col=c_up)}
    z_down = {0: virt(c, j, 0, col=c_down)}
    z_up[0] = virt(c, j, 0, col=c_up)
    z_down[1] = virt(c, j, 1, col=c_down)
    up = {1: slab(d, 1, depth=d_up)}
    down = {0: slab(d, 0, depth=d_down)}
    up[0] = slab(d, 0, depth=d_up)
    down[1] = slab(d, 1, depth=d_down)
    share = [send(vq.at[c], vq.at[c], col=c_sib)]

    rows_a, rows_b, rows_c = {}, {}, {}
    z_up[1].wait_recv()
    z_up2 = virt(c_down, j, 1, col=c_up)
    rows_a[1] = virt_rows(c_down, 1)
    z_down[0].wait_recv()
    z_down2 = virt(c_up, j, 0, col=c_down)
    rows_b[0] = virt_rows(c_up, 0)
    up2, down2 = {}, {}
    pair[1].wait_recv()
    up2[1] = slab(d_sib, 1, depth=d_up)
    pair[0].wait_recv()
    down2[0] = slab(d_sib, 0, depth=d_down)
    up2[0] = slab(d_sib, 0, depth=d_up)
    down2[1] = slab(d_sib, 1, depth=d_down)
    z_up[0].wait_recv()
    rows_a[0] = virt_rows(c_down, 0)
    z_down[1].wait_recv()
    rows_b[1] = virt_rows(c_up, 1)
    up[1].wait_recv()
    up3 = slab(d_down, 1, depth=d_up)
    down[0].wait_recv()
    down3 = slab(d_up, 0, depth=d_down)

    def pass_up(n, rows):
        rows[1][0].wait_recv()
        return virt(n, j_down, 1, row=r_up)

    def pass_down(n, rows):
        rows[0][1].wait_recv()
        return virt(n, j_up, 0, row=r_down)

    z_up2.wait_recv()
    rows_c[1] = virt_rows(c_far, 1)
    z_down2.wait_recv()
    rows_c[0] = virt_rows(c_far, 0)
    on_a = [pass_up(c_down, rows_a)]
    on_b = [pass_down(c_up, rows_b)]
    on_a.append(pass_down(c_down, rows_a))
    on_b.append(pass_up(c_up, rows_b))
    up2[1].wait_recv()
    up4 = slab(other(d_down), 1, depth=d_up)
    down2[0].wait_recv()
    down4 = slab(other(d_up), 0, depth=d_down)
    on_c = [pass_up(c_far, rows_c), pass_down(c_far, rows_c)]

    wrow[...] = jnp.zeros_like(wrow)
    freq = freq_in[0]
    for orbital in range(2):
        gap = energy_in[...] - occ_in[orbital]
        weight = 4.0 * gap / (gap * gap + freq * freq)
        wrow[:, 0:nvir] = jnp.broadcast_to(weight, (LANES, nvir))
        wcol[432 * orbital : 432 * orbital + 432, :] = wrow[...].T[0:nvir, :]
    acc[...] = jnp.zeros_like(acc)

    for n, rows, on in ((c_down, rows_a, on_a), (c_up, rows_b, on_b), (c_far, rows_c, on_c)):
        for copy in (rows[0][0], rows[1][1], *on):
            copy.wait_recv()
        share.append(send(vq.at[n], vq.at[n], col=c_sib))
    for copy in (up[0], down[1], up2[0], down2[1], up3, down3, up4, down4):
        copy.wait_recv()

    def couple(parity):
        @pl.loop(0, 4)
        def _(at):
            n = 2 * at + parity
            left = jnp.concatenate([vq[n, 0], vq[n, 1], vq[n, 2], vq[n, 3]], axis=1)
            right = jnp.concatenate([hs[n, 0], hs[n, 1]], axis=1)
            acc[...] += jnp.dot(left, right, preferred_element_type=F32)

    couple(lax.rem(c, 2))
    for copy in share:
        copy.wait_recv()
    couple(1 - lax.rem(c, 2))
    halves = (pl.ds(0, 432), pl.ds(432, 432))
    for orbital in range(2):
        rp[c, halves[orbital], :] = acc[:, LANES * orbital : LANES * orbital + LANES].astype(BF)

    def panel(n, half, **target):
        piece = rp.at[n, halves[half]]
        return send(piece, piece, **target)

    def piece_on(slot, half, to, **target):
        return send(qp.at[slot, halves[half]], qp.at[to, halves[half]], **target)

    y_up = {1: send(rp.at[c, halves[1]], qp.at[1, halves[1]], row=r_up)}
    y_down = {0: send(rp.at[c, halves[0]], qp.at[2, halves[0]], row=r_down)}
    z_up = {1: panel(c, 1, col=c_up)}
    z_down = {0: panel(c, 0, col=c_down)}
    y_up[0] = send(rp.at[c, halves[0]], qp.at[1, halves[0]], row=r_up)
    y_down[1] = send(rp.at[c, halves[1]], qp.at[2, halves[1]], row=r_down)
    z_up[0] = panel(c, 0, col=c_up)
    z_down[1] = panel(c, 1, col=c_down)
    share_own = send(rp.at[c], rp.at[c], col=c_sib)
    qp[0] = rp[c]

    def weigh(n):
        product = wcol[...] * rp[n].astype(F32)
        wl[n] = product.astype(BF).T

    weigh(c)
    y_up2, y_down2, y_up3, y_down3 = {}, {}, {}, {}

    def y_step(before_up, before_down, after_up, after_down, slot):
        for half in (1, 0):
            before_up[half].wait_recv()
            after_up[half] = piece_on(slot, half, slot + 2, row=r_up)
            before_down[1 - half].wait_recv()
            after_down[1 - half] = piece_on(slot + 1, 1 - half, slot + 3, row=r_down)

    z_up[1].wait_recv()
    z_up2 = panel(c_down, 1, col=c_up)
    z_down[0].wait_recv()
    z_down2 = panel(c_up, 0, col=c_down)
    y_step(y_up, y_down, y_up2, y_down2, 1)
    z_up[0].wait_recv()
    share_down = send(rp.at[c_down], rp.at[c_down], col=c_sib)
    z_down[1].wait_recv()
    share_up = send(rp.at[c_up], rp.at[c_up], col=c_sib)
    share_own.wait_recv()
    weigh(c_sib)
    weigh(c_down)
    y_step(y_up2, y_down2, y_up3, y_down3, 3)
    weigh(c_up)
    z_up2.wait_recv()
    z_down2.wait_recv()
    share_far = send(rp.at[c_far], rp.at[c_far], col=c_sib)
    share_down.wait_recv()
    weigh(other(c_down))
    y_up3[1].wait_recv()
    y_up4 = piece_on(5, 1, 7, row=r_up)
    y_down3[0].wait_recv()
    y_down4 = piece_on(6, 0, 7, row=r_down)
    share_up.wait_recv()
    weigh(other(c_up))
    weigh(c_far)
    share_far.wait_recv()
    weigh(other(c_far))

    low, high = slice(0, 64), slice(64, 128)
    targets = {"far": d_far, "up": d_up, "down": d_down, "own": d}

    def terms_of(name, slots):
        rows = wl[pl.ds(2 * (targets[name] // 2), 2)].reshape(256, 864)
        columns = jnp.concatenate([qp[slot] for slot in slots], axis=1)
        terms = jnp.dot(rows, columns, preferred_element_type=F32)
        return terms.reshape(2, 128, LANES * len(slots))

    class RingSum:
        def __init__(self, raw, land, keep, own):
            self.raw, self.land, self.keep, self.own, self.copies = raw, land, keep, own, {}

        def send(self, at, value, **target):
            self.raw[at] = value.astype(BF)
            self.copies[at] = send(self.raw.at[at], self.land.at[at], **target)

        def give(self, name, block):
            if name == "far":
                self.send(0, block[:, high], depth=d_up)
                self.send(1, block[:, low], depth=d_down)
            elif name == "up":
                self.send(2, block[:, low], depth=d_up)
                self.keep[0] = block[:, high]
            elif name == "down":
                self.send(3, block[:, high], depth=d_down)
                self.keep[1] = block[:, low]
            else:
                self.own[...] = block

        def pass_on(self):
            for at, target in ((0, d_up), (1, d_down)):
                self.copies[at].wait_recv()
                self.send(at + 4, self.keep[at] + self.land[at].astype(F32), depth=target)

        def end(self):
            for at in (2, 3, 4, 5):
                self.copies[at].wait_recv()
            land = self.land
            self.own[:, low] = self.own[:, low] + land[2].astype(F32) + land[5].astype(F32)
            self.own[:, high] = self.own[:, high] + land[3].astype(F32) + land[4].astype(F32)

    plane = lax.rem(d, 2)
    slots_a, slots_b = (0, 1, 2, 3, 4), (5, 6, 7)
    ring_a = RingSum(a_raw, a_land, a_keep, a_own)
    ring_b = RingSum(b_raw, b_land, b_keep, b_own)
    for name in targets:
        ring_a.give(name, terms_of(name, slots_a))
    ring_a.pass_on()
    y_up3[0].wait_recv()
    y_down3[1].wait_recv()
    y_up4.wait_recv()
    y_down4.wait_recv()
    b_pair = {}
    for at, name in enumerate(targets):
        b_terms[at] = terms_of(name, slots_b)
        b_give[at] = b_terms[at, 1 - plane].astype(BF)
        b_pair[name] = send(b_give.at[at], b_take.at[at], depth=d_sib)
    ring_a.end()
    a_sib[...] = a_own[1 - plane].astype(BF)
    last = send(a_sib, a_last, depth=d_sib)
    for at, name in enumerate(targets):
        b_pair[name].wait_recv()
        ring_b.give(name, (b_terms[at, plane] + b_take[at].astype(F32))[None])

    rows_of = [r, r_down, r_up, *(lax.rem(r + step, RING) for step in (6, 2, 5, 3, 4))]

    def tile(at):
        return pl.ds(pl.multiple_of(at * LANES, LANES), LANES)

    def in_first(at):
        apart = lax.rem(at - r + RING, RING)
        return jnp.logical_or(apart <= 2, apart >= 6)

    last.wait_recv()
    total = (a_own[plane] + a_last[...].astype(F32)).astype(BF)
    for at, slot in enumerate(slots_a):
        red[rows_of[slot]] = total[:, LANES * at : LANES * at + LANES]
    spread = []
    for step in (4, 2, 6, 3, 5, 1, 7):
        to = lax.rem(c + step, RING)
        copy = links.plan(red.at[to], out_ref.at[d, :, tile(c)], col=to)
        spread.append((to, copy))
        pl.when(in_first(to))(copy.start)
    ring_b.pass_on()
    ring_b.end()
    for at, slot in enumerate(slots_b):
        red[rows_of[slot]] = b_own[0, :, LANES * at : LANES * at + LANES].astype(BF)
    for to, copy in spread:
        pl.when(jnp.logical_not(in_first(to)))(copy.start)
    out_ref[d, :, tile(c)] = red[c]
    for _, copy in spread:
        copy.wait_recv()

    def part(n, begin, size):
        return out_ref.at[n, pl.ds(begin, size)]

    def pass_on(n, begin, size, **target):
        return send(part(n, begin, size), part(n, begin, size), **target)

    pair = pass_on(d, 0, 64, depth=d_sib)
    b_up = pass_on(d, 64, 64, depth=d_up)
    b_down = pass_on(d, 64, 64, depth=d_down)
    b_pairs = [pass_on(d, 64, 64, depth=d_sib)]
    a_up = pass_on(d, 0, 64, depth=d_up)
    a_down = pass_on(d, 0, 64, depth=d_down)
    pair.wait_recv()
    a_up2 = pass_on(d_sib, 0, 64, depth=d_up)
    a_down2 = pass_on(d_sib, 0, 64, depth=d_down)
    b_up.wait_recv()
    b_up2 = pass_on(d_down, 96, 32, depth=d_up)
    b_pairs.append(pass_on(d_down, 64, 64, depth=d_sib))
    b_down.wait_recv()
    b_down2 = pass_on(d_up, 64, 32, depth=d_down)
    b_pairs.append(pass_on(d_up, 64, 64, depth=d_sib))
    a_up.wait_recv()
    a_up3 = pass_on(d_down, 32, 32, depth=d_up)
    a_down.wait_recv()
    a_down3 = pass_on(d_up, 0, 32, depth=d_down)
    b_up2.wait_recv()
    b_pairs.append(pass_on(d_far, 96, 32, depth=d_sib))
    b_down2.wait_recv()
    b_pairs.append(pass_on(d_far, 64, 32, depth=d_sib))
    a_up2.wait_recv()
    a_up4 = pass_on(other(d_down), 32, 32, depth=d_up)
    a_down2.wait_recv()
    a_down4 = pass_on(other(d_up), 0, 32, depth=d_down)
    for copy in (a_up3, a_down3, a_up4, a_down4, *b_pairs):
        copy.wait_recv()
    links.finish()


def on_device(half_slabs, virtuals, occupied_energy, virtual_energy, frequency):
    hbm = pl.BlockSpec(memory_space=pltpu.HBM)
    copies = 120
    gram = pl.pallas_call(
        gather_kernel,
        out_shape=jax.ShapeDtypeStruct((RING, 128, 1024), BF),
        in_specs=[hbm] * 5,
        out_specs=pl.BlockSpec(memory_space=pltpu.VMEM),
        scratch_shapes=[
            pltpu.VMEM((2, 500, LANES), BF),
            pltpu.VMEM((500, 432), BF),
            pltpu.VMEM((1, 432), F32),
            pltpu.SMEM((2,), F32),
            pltpu.SMEM((1,), F32),
            pltpu.VMEM((512, 512), BF),
            pltpu.VMEM((RING, 4, 432, LANES), BF),
            pltpu.VMEM((RING, 2, 512, LANES), BF),
            pltpu.VMEM((432, 2 * LANES), F32),
            pltpu.VMEM((RING, 864, LANES), BF),
            pltpu.VMEM((RING, 864, LANES), BF),
            pltpu.VMEM((LANES, 512), F32),
            pltpu.VMEM((864, LANES), F32),
            pltpu.VMEM((RING, 128, 864), BF),
            pltpu.VMEM((6, 2, 64, 640), BF),
            pltpu.VMEM((6, 2, 64, 640), BF),
            pltpu.VMEM((2, 2, 64, 640), F32),
            pltpu.VMEM((2, 128, 640), F32),
            pltpu.VMEM((128, 640), BF),
            pltpu.VMEM((128, 640), BF),
            pltpu.VMEM((4, 2, 128, 384), F32),
            pltpu.VMEM((6, 1, 64, 384), BF),
            pltpu.VMEM((6, 1, 64, 384), BF),
            pltpu.VMEM((2, 1, 64, 384), F32),
            pltpu.VMEM((1, 128, 384), F32),
            pltpu.VMEM((4, 128, 384), BF),
            pltpu.VMEM((4, 128, 384), BF),
            pltpu.VMEM((RING, 128, LANES), BF),
            pltpu.SemaphoreType.DMA((5,)),
            pltpu.SemaphoreType.DMA((copies,)),
            pltpu.SemaphoreType.DMA((copies,)),
        ],
        compiler_params=pltpu.CompilerParams(
            collective_id=0, has_side_effects=True, vmem_limit_bytes=48 * 2**20
        ),
        cost_estimate=pl.CostEstimate(flops=2_700_000_000, bytes_accessed=3_000_000, transcendentals=0),
    )(half_slabs, virtuals, virtual_energy.reshape(1, -1), occupied_energy, frequency)
    return gram.reshape(1024, 1024).astype(F32)


def solution(mesh):
    placed = (P(None, "depth", ("row", "col")), P("col", "depth"), P(), P("depth"), P())
    return jax.shard_map(
        on_device, mesh=mesh, in_specs=placed, out_specs=P("row", "col"), check_vma=False
    )
```

time: 463 us -> 118 us (0.25)
  the two profiles are of different devices: /device:TPU:1 before, /device:TPU:33 now
where the time goes in v1:
time: 118 us
  Pallas kernels  111 us (94%)
  local copies, waits for them, and re-layouts  3.53 us (3%)
  other arithmetic  2.61 us (2%)
    pallas_call x1, Pallas kernels, on_device(): pl.pallas_call(gather_kernel, out_shape=jax.ShapeDtypeStruct((RING, 128,...  111 us
    unnamed x6, local copies, waits for them, and re-layouts  3.53 us
    convert_element_type x1, other arithmetic, on_device(): return gram.reshape(1024, 1024).astype(F32)  2.61 us

profile of v1, /device:TPU:33, one launch (start us, length us, event | category | flops | bytes accessed | tf_op | source)
XLA Modules:
  0.0 118.2 jit_solution(2716933890763822167)
XLA Ops:
  0.7 1.0 copy.6.slabs_ref
  1.6 1.2 %copy.7.virt_ref = bf16[500,432]{1,0:T(8,128)(2,1)S(1)} copy(bf16[500,432]{0,1:T(8,128)(2,1)} %param.6) | data formatting | bytes 864000 | tf_op args[1]
  2.9 0.0 copy-start
  2.9 0.7 copy-done
  3.5 0.0 copy-start.1
  3.5 0.7 copy-done.1
  4.2 111.4 %shard_map.55 = bf16[8,128,1024]{2,1,0:T(8,128)(2,1)S(1)} custom-call(bf16[2,500,128]{2,1,0:T(8,128)(2,1)S(1)} %copy.6.slabs_ref, bf16[500,432]{1,0:T(8,128)(2,1)S(1)} %copy.7.virt_ref, f32[1,432]{1,0:T(1,128)S(1)} %bitcast.4, f32[2]{0:T(128)S(1)} %copy-done.1, f32[1]{0:T(128)S(6)} %copy.8.freq_ref), custom_call_target="tpu_custom_call" | custom-call | flops 2700000000 | bytes 3000000 | tf_op jit(solution)/shard_map/pallas_call | solution.py:394
  115.6 2.6 %bitcast_convert_fusion = f32[1024,1024]{1,0:T(8,128)} fusion(bf16[8,128,1024]{2,1,0:T(8,128)(2,1)S(1)} %shard_map.55), kind=kLoop, calls=%fused_computation | loop fusion | flops 1048576 | bytes 6291456 | tf_op jit(solution)/shard_map/convert_element_type | solution.py:437
Async XLA Ops:
  2.9 0.7 copy-start
  3.5 0.7 copy-start.1

commit v2 on v1

v2 whole, which is shorter than its diff:
```python
import jax
import jax.numpy as jnp
from jax import lax
from jax.experimental import pallas as pl
from jax.experimental.pallas import tpu as pltpu
from jax.sharding import PartitionSpec as P

MESH = pl.DeviceIdType.MESH
BF = jnp.bfloat16
F32 = jnp.float32
RING = 8
LANES = 128


class Links:
    def __init__(self, send_sems, recv_sems):
        self.send_sems, self.recv_sems, self.copies = send_sems, recv_sems, []

    def plan(self, src, dst, **target):
        at = len(self.copies)
        copy = pltpu.make_async_remote_copy(
            src_ref=src,
            dst_ref=dst,
            send_sem=self.send_sems.at[at],
            recv_sem=self.recv_sems.at[at],
            device_id=target,
            device_id_type=MESH,
        )
        self.copies.append(copy)
        return copy

    def send(self, src, dst, **target):
        copy = self.plan(src, dst, **target)
        copy.start()
        return copy

    def finish(self):
        for copy in self.copies:
            copy.wait_send()


def around(me):
    up, down, far = lax.rem(me + 2, RING), lax.rem(me + 6, RING), lax.rem(me + 4, RING)
    return up, down, far, me + 1 - 2 * lax.rem(me, 2)


def other(at):
    return at + 1 - 2 * lax.rem(at, 2)


def gather_kernel(
    slabs_ref, virt_ref, weight_ref, out_ref,
    slab_in, virt_in, weight_in, vq, hs, acc, rp, qp, wrow, wcol, wl,
    a_raw, a_land, a_keep, a_own, a_sib, a_last,
    b_terms, b_raw, b_land, b_keep, b_own, b_give, b_take, red,
    local_sems, send_sems, recv_sems,
):
    d, r, c = lax.axis_index("depth"), lax.axis_index("row"), lax.axis_index("col")
    d_up, d_down, d_far, d_sib = around(d)
    c_up, c_down, c_far, c_sib = around(c)
    r_up, r_down = lax.rem(r + 1, RING), lax.rem(r + 7, RING)
    links = Links(send_sems, recv_sems)
    send = links.send

    loads = [
        pltpu.make_async_copy(src, dst, local_sems.at[at])
        for at, (src, dst) in enumerate(((virt_ref, virt_in), (slabs_ref, slab_in), (weight_ref, weight_in)))
    ]
    for load in loads:
        load.start()
    barrier = pltpu.get_barrier_semaphore()
    partners = [{"depth": d_up}, {"depth": d_down}, {"depth": d_sib}, {"row": r_up}, {"row": r_down}]
    partners += [{"col": lax.rem(c + step, RING)} for step in range(1, RING)]
    for partner in partners:
        pl.semaphore_signal(barrier, inc=1, device_id=partner, device_id_type=MESH)

    nvir, nbas = virt_ref.shape
    vq[c, 3] = jnp.zeros((nvir, LANES), BF)
    for load in loads:
        load.wait()
    for quarter in range(3):
        vq[c, quarter] = virt_in[:, LANES * quarter : LANES * quarter + LANES]
    vq[c, 3, :, 0 : nbas - 384] = virt_in[:, 384:nbas]
    for orbital in range(2):
        hs[d, orbital, 496:512, :] = jnp.zeros((16, LANES), BF)
        hs[d, orbital, 0:nbas, :] = slab_in[orbital]

    pl.semaphore_wait(barrier, len(partners))

    j = lax.rem(r, 4)
    j_up, j_down = lax.rem(j + 1, 4), lax.rem(j + 3, 4)
    spans = (pl.ds(0, 208), pl.ds(208, 224))

    def slab(n, orbital, half=None, **target):
        piece = hs.at[n, orbital] if half is None else hs.at[n, orbital, pl.ds(256 * half, 256)]
        return send(piece, piece, **target)

    def virt(n, quarter, half, **target):
        piece = vq.at[n, quarter, spans[half]]
        return send(piece, piece, **target)

    def virt_rows(n, half):
        return virt(n, j, half, row=r_up), virt(n, j, half, row=r_down)

    pair, up, down, up2, down2, up3, down3, up4, down4 = ({} for _ in range(9))

    def slabs_out(o):
        up[o], down[o] = slab(d, o, depth=d_up), slab(d, o, depth=d_down)

    def slabs_sib(o):
        pair[o].wait_recv()
        up2[o], down2[o] = slab(d_sib, o, depth=d_up), slab(d_sib, o, depth=d_down)

    def slabs_on(o):
        up[o].wait_recv()
        up3[o] = slab(d_down, o, 1, depth=d_up)
        down[o].wait_recv()
        down3[o] = slab(d_up, o, 0, depth=d_down)

    def slabs_sib_on(o):
        up2[o].wait_recv()
        up4[o] = slab(other(d_down), o, 1, depth=d_up)
        down2[o].wait_recv()
        down4[o] = slab(other(d_up), o, 0, depth=d_down)

    def slabs_end(o):
        for copy in (up3[o], down3[o], up4[o], down4[o]):
            copy.wait_recv()

    z_up = {1: virt(c, j, 1, col=c_up)}
    z_down = {0: virt(c, j, 0, col=c_down)}
    z_up[0] = virt(c, j, 0, col=c_up)
    z_down[1] = virt(c, j, 1, col=c_down)
    slabs_out(0)
    pair[0] = slab(d, 0, depth=d_sib)
    share_own = send(vq.at[c], vq.at[c], col=c_sib)

    rows_a, rows_b, rows_c = {}, {}, {}
    z_up[1].wait_recv()
    z_up2 = virt(c_down, j, 1, col=c_up)
    rows_a[1] = virt_rows(c_down, 1)
    z_down[0].wait_recv()
    z_down2 = virt(c_up, j, 0, col=c_down)
    rows_b[0] = virt_rows(c_up, 0)
    z_up[0].wait_recv()
    rows_a[0] = virt_rows(c_down, 0)
    z_down[1].wait_recv()
    rows_b[1] = virt_rows(c_up, 1)
    slabs_sib(0)
    slabs_on(0)
    z_up2.wait_recv()
    rows_c[1] = virt_rows(c_far, 1)
    z_down2.wait_recv()
    rows_c[0] = virt_rows(c_far, 0)
    pair[1] = slab(d, 1, depth=d_sib)
    slabs_out(1)

    def pass_up(n, rows):
        rows[1][0].wait_recv()
        return virt(n, j_down, 1, row=r_up)

    def pass_down(n, rows):
        rows[0][1].wait_recv()
        return virt(n, j_up, 0, row=r_down)

    on_a = [pass_up(c_down, rows_a)]
    on_b = [pass_down(c_up, rows_b)]
    on_a.append(pass_down(c_down, rows_a))
    on_b.append(pass_up(c_up, rows_b))
    slabs_sib_on(0)
    on_c = [pass_up(c_far, rows_c), pass_down(c_far, rows_c)]
    slabs_sib(1)
    slabs_on(1)

    wrow[...] = jnp.zeros_like(wrow)
    for orbital in range(2):
        wrow[:, 0:nvir] = jnp.broadcast_to(weight_in[orbital : orbital + 1, :], (LANES, nvir))
        wcol[orbital] = wrow[...].T[0:nvir, :]
    acc[...] = jnp.zeros_like(acc)

    def virt_end(n, rows, on):
        for copy in (rows[0][0], rows[1][1], *on):
            copy.wait_recv()
        return send(vq.at[n], vq.at[n], col=c_sib)

    def couple(n, orbital):
        left = jnp.concatenate([vq[n, 0], vq[n, 1], vq[n, 2], vq[n, 3]], axis=1)
        acc[orbital] += jnp.dot(left, hs[n, orbital], preferred_element_type=F32)

    share_a = virt_end(c_down, rows_a, on_a)
    share_b = virt_end(c_up, rows_b, on_b)
    slabs_end(0)
    couple(c, 0)
    share_own.wait_recv()
    couple(c_sib, 0)
    couple(c_down, 0)
    couple(c_up, 0)
    share_c = virt_end(c_far, rows_c, on_c)
    slabs_sib_on(1)
    share_a.wait_recv()
    couple(other(c_down), 0)
    share_b.wait_recv()
    couple(other(c_up), 0)
    couple(c_far, 0)
    share_c.wait_recv()
    couple(other(c_far), 0)

    def panel(n, orbital, **target):
        return send(rp.at[n, orbital], rp.at[n, orbital], **target)

    y_up, y_down, z_up, z_down = {}, {}, {}, {}
    share_own, share_down, share_up, share_far = {}, {}, {}, {}

    def panels_out(o):
        rp[c, o] = acc[o].astype(BF)
        y_up[1, o] = send(rp.at[c, o], qp.at[1, o], row=r_up)
        y_down[1, o] = send(rp.at[c, o], qp.at[2, o], row=r_down)
        z_up[o] = panel(c, o, col=c_up)
        z_down[o] = panel(c, o, col=c_down)
        share_own[o] = panel(c, o, col=c_sib)
        qp[0, o] = rp[c, o]

    def y_step(step, o):
        slot = 2 * step - 1
        y_up[step, o].wait_recv()
        y_up[step + 1, o] = send(qp.at[slot, o], qp.at[slot + 2, o], row=r_up)
        y_down[step, o].wait_recv()
        y_down[step + 1, o] = send(qp.at[slot + 1, o], qp.at[slot + 3, o], row=r_down)

    def z_step(o):
        z_up[o].wait_recv()
        if o == 1:
            z_up["far"] = panel(c_down, 1, col=c_up)
        share_down[o] = panel(c_down, o, col=c_sib)
        z_down[o].wait_recv()
        if o == 0:
            z_down["far"] = panel(c_up, 0, col=c_down)
        share_up[o] = panel(c_up, o, col=c_sib)

    def weigh(n, o):
        product = wcol[o] * rp[n, o].astype(F32)
        wl[o, n] = product.astype(BF).T

    panels_out(0)
    slabs_end(1)

    @pl.loop(0, RING)
    def _(n):
        couple(n, 1)

    panels_out(1)
    y_step(1, 0)
    z_step(0)
    weigh(c, 0)
    weigh(c, 1)
    y_step(1, 1)
    z_step(1)
    share_own[0].wait_recv()
    weigh(c_sib, 0)
    weigh(c_down, 0)
    y_step(2, 0)
    weigh(c_up, 0)
    z_down["far"].wait_recv()
    share_far[0] = panel(c_far, 0, col=c_sib)
    share_own[1].wait_recv()
    weigh(c_sib, 1)
    y_step(2, 1)
    weigh(c_down, 1)
    z_up["far"].wait_recv()
    share_far[1] = panel(c_far, 1, col=c_sib)
    weigh(c_up, 1)
    weigh(c_far, 0)
    for n, share in ((other(c_down), share_down), (other(c_up), share_up)):
        share[0].wait_recv()
        weigh(n, 0)
    y_down[3, 0].wait_recv()
    y_down[4, 0] = send(qp.at[6, 0], qp.at[7, 0], row=r_down)
    for n, share in ((other(c_down), share_down), (other(c_up), share_up)):
        share[1].wait_recv()
        weigh(n, 1)
    y_up[3, 1].wait_recv()
    y_up[4, 1] = send(qp.at[5, 1], qp.at[7, 1], row=r_up)
    weigh(c_far, 1)
    for o in range(2):
        share_far[o].wait_recv()
        weigh(other(c_far), o)

    low, high = slice(0, 64), slice(64, 128)
    targets = {"far": d_far, "up": d_up, "down": d_down, "own": d}

    def terms_of(name, slots):
        terms = 0.0
        for o in range(2):
            rows = wl[o, pl.ds(2 * (targets[name] // 2), 2)].reshape(256, 432)
            columns = jnp.concatenate([qp[slot, o] for slot in slots], axis=1)
            terms += jnp.dot(rows, columns, preferred_element_type=F32)
        return terms.reshape(2, 128, LANES * len(slots))

    class RingSum:
        def __init__(self, raw, land, keep, own):
            self.raw, self.land, self.keep, self.own, self.copies = raw, land, keep, own, {}

        def send(self, at, value, **target):
            self.raw[at] = value.astype(BF)
            self.copies[at] = send(self.raw.at[at], self.land.at[at], **target)

        def give(self, name, block):
            if name == "far":
                self.send(0, block[:, high], depth=d_up)
                self.send(1, block[:, low], depth=d_down)
            elif name == "up":
                self.send(2, block[:, low], depth=d_up)
                self.keep[0] = block[:, high]
            elif name == "down":
                self.send(3, block[:, high], depth=d_down)
                self.keep[1] = block[:, low]
            else:
                self.own[...] = block

        def pass_on(self):
            for at, target in ((0, d_up), (1, d_down)):
                self.copies[at].wait_recv()
                self.send(at + 4, self.keep[at] + self.land[at].astype(F32), depth=target)

        def end(self):
            for at in (2, 3, 4, 5):
                self.copies[at].wait_recv()
            land = self.land
            self.own[:, low] = self.own[:, low] + land[2].astype(F32) + land[5].astype(F32)
            self.own[:, high] = self.own[:, high] + land[3].astype(F32) + land[4].astype(F32)

    plane = lax.rem(d, 2)
    slots_a, slots_b = (0, 1, 2, 3, 4), (5, 6, 7)
    ring_a = RingSum(a_raw, a_land, a_keep, a_own)
    ring_b = RingSum(b_raw, b_land, b_keep, b_own)
    for name in targets:
        ring_a.give(name, terms_of(name, slots_a))
    y_up[3, 0].wait_recv()
    y_down[3, 1].wait_recv()
    y_up[4, 1].wait_recv()
    y_down[4, 0].wait_recv()
    b_pair = {}
    for at, name in enumerate(targets):
        b_terms[at] = terms_of(name, slots_b)
        b_give[at] = b_terms[at, 1 - plane].astype(BF)
        b_pair[name] = send(b_give.at[at], b_take.at[at], depth=d_sib)
        if at == 0:
            ring_a.pass_on()
    for at, name in enumerate(targets):
        b_pair[name].wait_recv()
        ring_b.give(name, (b_terms[at, plane] + b_take[at].astype(F32))[None])
    ring_a.end()
    a_sib[...] = a_own[1 - plane].astype(BF)
    last = send(a_sib, a_last, depth=d_sib)
    ring_b.pass_on()

    rows_of = [r, r_down, r_up, *(lax.rem(r + step, RING) for step in (6, 2, 5, 3, 4))]

    def tile(at):
        return pl.ds(pl.multiple_of(at * LANES, LANES), LANES)

    def in_first(at):
        apart = lax.rem(at - r + RING, RING)
        return jnp.logical_or(apart <= 2, apart >= 6)

    last.wait_recv()
    total = (a_own[plane] + a_last[...].astype(F32)).astype(BF)
    for at, slot in enumerate(slots_a):
        red[rows_of[slot]] = total[:, LANES * at : LANES * at + LANES]
    spread = []
    for step in (4, 2, 6, 3, 5, 1, 7):
        to = lax.rem(c + step, RING)
        copy = links.plan(red.at[to], out_ref.at[d, :, tile(c)], col=to)
        spread.append((to, copy))
        pl.when(in_first(to))(copy.start)
    ring_b.end()
    for at, slot in enumerate(slots_b):
        red[rows_of[slot]] = b_own[0, :, LANES * at : LANES * at + LANES].astype(BF)
    for to, copy in spread:
        pl.when(jnp.logical_not(in_first(to)))(copy.start)
    out_ref[d, :, tile(c)] = red[c]
    for _, copy in spread:
        copy.wait_recv()

    def part(n, begin, size):
        return out_ref.at[n, pl.ds(begin, size)]

    def pass_on(n, begin, size, **target):
        return send(part(n, begin, size), part(n, begin, size), **target)

    pair = pass_on(d, 0, 64, depth=d_sib)
    b_up = pass_on(d, 64, 64, depth=d_up)
    b_down = pass_on(d, 64, 64, depth=d_down)
    b_pairs = [pass_on(d, 64, 64, depth=d_sib)]
    a_up = pass_on(d, 0, 64, depth=d_up)
    a_down = pass_on(d, 0, 64, depth=d_down)
    pair.wait_recv()
    a_up2 = pass_on(d_sib, 0, 64, depth=d_up)
    a_down2 = pass_on(d_sib, 0, 64, depth=d_down)
    b_up.wait_recv()
    b_up2 = pass_on(d_down, 96, 32, depth=d_up)
    b_pairs.append(pass_on(d_down, 64, 64, depth=d_sib))
    b_down.wait_recv()
    b_down2 = pass_on(d_up, 64, 32, depth=d_down)
    b_pairs.append(pass_on(d_up, 64, 64, depth=d_sib))
    a_up.wait_recv()
    a_up3 = pass_on(d_down, 32, 32, depth=d_up)
    a_down.wait_recv()
    a_down3 = pass_on(d_up, 0, 32, depth=d_down)
    b_up2.wait_recv()
    b_pairs.append(pass_on(d_far, 96, 32, depth=d_sib))
    b_down2.wait_recv()
    b_pairs.append(pass_on(d_far, 64, 32, depth=d_sib))
    a_up2.wait_recv()
    a_up4 = pass_on(other(d_down), 32, 32, depth=d_up)
    a_down2.wait_recv()
    a_down4 = pass_on(other(d_up), 0, 32, depth=d_down)
    for copy in (a_up3, a_down3, a_up4, a_down4, *b_pairs):
        copy.wait_recv()
    links.finish()


def on_device(half_slabs, virtuals, occupied_energy, virtual_energy, frequency):
    hbm = pl.BlockSpec(memory_space=pltpu.HBM)
    excitation = virtual_energy[None, :] - occupied_energy[:, None]
    weight = 4.0 * excitation / (excitation * excitation + frequency[0] * frequency[0])
    copies = 128
    gram = pl.pallas_call(
        gather_kernel,
        out_shape=jax.ShapeDtypeStruct((RING, 128, 1024), BF),
        in_specs=[hbm] * 3,
        out_specs=pl.BlockSpec(memory_space=pltpu.VMEM),
        scratch_shapes=[
            pltpu.VMEM((2, 500, LANES), BF),
            pltpu.VMEM((432, 500), BF),
            pltpu.VMEM((2, 432), F32),
            pltpu.VMEM((RING, 4, 432, LANES), BF),
            pltpu.VMEM((RING, 2, 512, LANES), BF),
            pltpu.VMEM((2, 432, LANES), F32),
            pltpu.VMEM((RING, 2, 432, LANES), BF),
            pltpu.VMEM((RING, 2, 432, LANES), BF),
            pltpu.VMEM((LANES, 512), F32),
            pltpu.VMEM((2, 432, LANES), F32),
            pltpu.VMEM((2, RING, 128, 432), BF),
            pltpu.VMEM((6, 2, 64, 640), BF),
            pltpu.VMEM((6, 2, 64, 640), BF),
            pltpu.VMEM((2, 2, 64, 640), F32),
            pltpu.VMEM((2, 128, 640), F32),
            pltpu.VMEM((128, 640), BF),
            pltpu.VMEM((128, 640), BF),
            pltpu.VMEM((4, 2, 128, 384), F32),
            pltpu.VMEM((6, 1, 64, 384), BF),
            pltpu.VMEM((6, 1, 64, 384), BF),
            pltpu.VMEM((2, 1, 64, 384), F32),
            pltpu.VMEM((1, 128, 384), F32),
            pltpu.VMEM((4, 128, 384), BF),
            pltpu.VMEM((4, 128, 384), BF),
            pltpu.VMEM((RING, 128, LANES), BF),
            pltpu.SemaphoreType.DMA((3,)),
            pltpu.SemaphoreType.DMA((copies,)),
            pltpu.SemaphoreType.DMA((copies,)),
        ],
        compiler_params=pltpu.CompilerParams(
            collective_id=0, has_side_effects=True, vmem_limit_bytes=48 * 2**20
        ),
        cost_estimate=pl.CostEstimate(flops=2_700_000_000, bytes_accessed=3_000_000, transcendentals=0),
    )(half_slabs, virtuals.T, weight)
    return gram.reshape(1024, 1024).astype(F32)


def solution(mesh):
    placed = (P(None, "depth", ("row", "col")), P("col", "depth"), P(), P("depth"), P())
    return jax.shard_map(
        on_device, mesh=mesh, in_specs=placed, out_specs=P("row", "col"), check_vma=False
    )
```

time: 118 us -> 114 us (0.966)
  the two profiles are of different devices: /device:TPU:33 before, /device:TPU:1 now
where the time goes in v2:
time: 114 us
  Pallas kernels  108 us (95%)
  other arithmetic  3.38 us (3%)
  local copies, waits for them, and re-layouts  1.99 us (2%)
    pallas_call x1, Pallas kernels, on_device(): pl.pallas_call(gather_kernel, out_shape=jax.ShapeDtypeStruct((RING, 128,...  108 us
    convert_element_type x1, other arithmetic, on_device(): return gram.reshape(1024, 1024).astype(F32)  2.61 us

profile of v2, /device:TPU:1, one launch (start us, length us, event | category | flops | bytes accessed | tf_op | source)
XLA Modules:
  0.0 113.7 jit_solution(5647918269643923738)
XLA Ops:
  0.7 0.8 fusion.weight_ref
  1.4 1.0 copy.6.slabs_ref
  2.4 0.0 copy-start
  2.4 1.0 copy-done
  3.4 107.6 %shard_map.55 = bf16[8,128,1024]{2,1,0:T(8,128)(2,1)S(1)} custom-call(bf16[2,500,128]{2,1,0:T(8,128)(2,1)S(1)} %copy.6.slabs_ref, bf16[432,500]{1,0:T(8,128)(2,1)S(1)} %bitcast.5, f32[2,432]{1,0:T(2,128)S(1)} %fusion.weight_ref), custom_call_target="tpu_custom_call" | custom-call | flops 2700000000 | bytes 3000000 | tf_op jit(solution)/shard_map/pallas_call | solution.py:428
  111.1 2.6 %bitcast_convert_fusion = f32[1024,1024]{1,0:T(8,128)} fusion(bf16[8,128,1024]{2,1,0:T(8,128)(2,1)S(1)} %shard_map.55), kind=kLoop, calls=%fused_computation | loop fusion | flops 1048576 | bytes 6291456 | tf_op jit(solution)/shard_map/convert_element_type | solution.py:468
Async XLA Ops:
  2.4 1.0 copy-start

commit v3 on v2

--- a/solution.py
+++ b/solution.py
@@ -50,9 +50,9 @@
 
 def gather_kernel(
     slabs_ref, virt_ref, weight_ref, out_ref,
-    slab_in, virt_in, weight_in, vq, hs, acc, rp, qp, wrow, wcol, wl,
+    slab_in, virt_in, weight_in, vq, hs, acc, qp, wrow, wcol, heavy, wl_a, wl_b,
     a_raw, a_land, a_keep, a_own, a_sib, a_last,
-    b_terms, b_raw, b_land, b_keep, b_own, b_give, b_take, red,
+    b_terms, b_raw, b_land, b_keep, b_own, b_give, b_take, red, spread_land, relay,
     local_sems, send_sems, recv_sems,
 ):
     d, r, c = lax.axis_index("depth"), lax.axis_index("row"), lax.axis_index("col")
@@ -177,6 +177,9 @@
         wrow[:, 0:nvir] = jnp.broadcast_to(weight_in[orbital : orbital + 1, :], (LANES, nvir))
         wcol[orbital] = wrow[...].T[0:nvir, :]
     acc[...] = jnp.zeros_like(acc)
+    for slot in range(RING):
+        qp[slot, 864:896, :] = jnp.zeros((32, LANES), BF)
+    heavy[864:896, :] = jnp.zeros((32, LANES), BF)
 
     def virt_end(n, rows, on):
         for copy in (rows[0][0], rows[1][1], *on):
@@ -205,27 +208,40 @@
     share_c.wait_recv()
     couple(other(c_far), 0)
 
-    def panel(n, orbital, **target):
-        return send(rp.at[n, orbital], rp.at[n, orbital], **target)
+    parts = (pl.ds(0, 384), pl.ds(384, 480))
+    panels = (wl_a, wl_b)
+
+    def panel(n, part, **target):
+        piece = panels[part].at[n]
+        return send(piece, piece, **target)
+
+    def column(slot, to, part, **target):
+        return send(qp.at[slot, parts[part]], qp.at[to, parts[part]], **target)
 
     y_up, y_down, z_up, z_down = {}, {}, {}, {}
     share_own, share_down, share_up, share_far = {}, {}, {}, {}
 
     def panels_out(o):
-        rp[c, o] = acc[o].astype(BF)
-        y_up[1, o] = send(rp.at[c, o], qp.at[1, o], row=r_up)
-        y_down[1, o] = send(rp.at[c, o], qp.at[2, o], row=r_down)
+        rows = slice(432 * o, 432 * o + 432)
+        plain = acc[o].astype(BF)
+        qp[0, rows, :] = plain
+        y_up[1, o] = column(0, 1, o, row=r_up)
+        y_down[1, o] = column(0, 2, o, row=r_down)
+        heavy[rows, :] = (wcol[o] * plain.astype(F32)).astype(BF)
+        if o == 0:
+            wl_a[c] = heavy[0:384, :].T
+        else:
+            wl_b[c] = heavy[384:896, :].T
         z_up[o] = panel(c, o, col=c_up)
         z_down[o] = panel(c, o, col=c_down)
         share_own[o] = panel(c, o, col=c_sib)
-        qp[0, o] = rp[c, o]
 
     def y_step(step, o):
         slot = 2 * step - 1
         y_up[step, o].wait_recv()
-        y_up[step + 1, o] = send(qp.at[slot, o], qp.at[slot + 2, o], row=r_up)
+        y_up[step + 1, o] = column(slot, slot + 2, o, row=r_up)
         y_down[step, o].wait_recv()
-        y_down[step + 1, o] = send(qp.at[slot + 1, o], qp.at[slot + 3, o], row=r_down)
+        y_down[step + 1, o] = column(slot + 1, slot + 3, o, row=r_down)
 
     def z_step(o):
         z_up[o].wait_recv()
@@ -237,10 +253,6 @@
             z_down["far"] = panel(c_up, 0, col=c_down)
         share_up[o] = panel(c_up, o, col=c_sib)
 
-    def weigh(n, o):
-        product = wcol[o] * rp[n, o].astype(F32)
-        wl[o, n] = product.astype(BF).T
-
     panels_out(0)
     slabs_end(1)
 
@@ -251,49 +263,30 @@
     panels_out(1)
     y_step(1, 0)
     z_step(0)
-    weigh(c, 0)
-    weigh(c, 1)
     y_step(1, 1)
     z_step(1)
-    share_own[0].wait_recv()
-    weigh(c_sib, 0)
-    weigh(c_down, 0)
     y_step(2, 0)
-    weigh(c_up, 0)
     z_down["far"].wait_recv()
     share_far[0] = panel(c_far, 0, col=c_sib)
-    share_own[1].wait_recv()
-    weigh(c_sib, 1)
     y_step(2, 1)
-    weigh(c_down, 1)
     z_up["far"].wait_recv()
     share_far[1] = panel(c_far, 1, col=c_sib)
-    weigh(c_up, 1)
-    weigh(c_far, 0)
-    for n, share in ((other(c_down), share_down), (other(c_up), share_up)):
+    for share in (share_own, share_down, share_up):
         share[0].wait_recv()
-        weigh(n, 0)
+        share[1].wait_recv()
     y_down[3, 0].wait_recv()
-    y_down[4, 0] = send(qp.at[6, 0], qp.at[7, 0], row=r_down)
-    for n, share in ((other(c_down), share_down), (other(c_up), share_up)):
-        share[1].wait_recv()
-        weigh(n, 1)
-    y_up[3, 1].wait_recv()
-    y_up[4, 1] = send(qp.at[5, 1], qp.at[7, 1], row=r_up)
-    weigh(c_far, 1)
-    for o in range(2):
-        share_far[o].wait_recv()
-        weigh(other(c_far), o)
+    y_down[4, 0] = column(6, 7, 0, row=r_down)
+    share_far[0].wait_recv()
+    share_far[1].wait_recv()
 
     low, high = slice(0, 64), slice(64, 128)
     targets = {"far": d_far, "up": d_up, "down": d_down, "own": d}
 
     def terms_of(name, slots):
-        terms = 0.0
-        for o in range(2):
-            rows = wl[o, pl.ds(2 * (targets[name] // 2), 2)].reshape(256, 432)
-            columns = jnp.concatenate([qp[slot, o] for slot in slots], axis=1)
-            terms += jnp.dot(rows, columns, preferred_element_type=F32)
+        at = pl.ds(2 * (targets[name] // 2), 2)
+        rows = jnp.concatenate([wl_a[at].reshape(256, 384), wl_b[at].reshape(256, 512)], axis=1)
+        columns = jnp.concatenate([qp[slot] for slot in slots], axis=1)
+        terms = jnp.dot(rows, columns, preferred_element_type=F32)
         return terms.reshape(2, 128, LANES * len(slots))
 
     class RingSum:
@@ -333,7 +326,10 @@
     slots_a, slots_b = (0, 1, 2, 3, 4), (5, 6, 7)
     ring_a = RingSum(a_raw, a_land, a_keep, a_own)
     ring_b = RingSum(b_raw, b_land, b_keep, b_own)
-    for name in targets:
+    ring_a.give("far", terms_of("far", slots_a))
+    y_up[3, 1].wait_recv()
+    y_up[4, 1] = column(5, 7, 1, row=r_up)
+    for name in ("up", "down", "own"):
         ring_a.give(name, terms_of(name, slots_a))
     y_up[3, 0].wait_recv()
     y_down[3, 1].wait_recv()
@@ -356,9 +352,6 @@
 
     rows_of = [r, r_down, r_up, *(lax.rem(r + step, RING) for step in (6, 2, 5, 3, 4))]
 
-    def tile(at):
-        return pl.ds(pl.multiple_of(at * LANES, LANES), LANES)
-
     def in_first(at):
         apart = lax.rem(at - r + RING, RING)
         return jnp.logical_or(apart <= 2, apart >= 6)
@@ -368,9 +361,15 @@
     for at, slot in enumerate(slots_a):
         red[rows_of[slot]] = total[:, LANES * at : LANES * at + LANES]
     spread = []
-    for step in (4, 2, 6, 3, 5, 1, 7):
-        to = lax.rem(c + step, RING)
-        copy = links.plan(red.at[to], out_ref.at[d, :, tile(c)], col=to)
+    far_sib = other(c_far)
+    for to, by in (
+        (c_far, c_up), (far_sib, c_down), (c_up, None), (c_down, None),
+        (other(c_up), None), (other(c_down), None), (c_sib, None),
+    ):
+        if by is None:
+            copy = links.plan(red.at[to], spread_land.at[c], col=to)
+        else:
+            copy = links.plan(red.at[to], relay.at[len(spread)], col=by)
         spread.append((to, copy))
         pl.when(in_first(to))(copy.start)
     ring_b.end()
@@ -378,9 +377,17 @@
         red[rows_of[slot]] = b_own[0, :, LANES * at : LANES * at + LANES].astype(BF)
     for to, copy in spread:
         pl.when(jnp.logical_not(in_first(to)))(copy.start)
-    out_ref[d, :, tile(c)] = red[c]
-    for _, copy in spread:
+    spread_land[c] = red[c]
+    spread[0][1].wait_recv()
+    relayed = [send(relay.at[0], spread_land.at[c_down], col=c_up)]
+    spread[1][1].wait_recv()
+    relayed.append(send(relay.at[1], spread_land.at[c_up], col=other(c_down)))
+    for _, copy in spread[2:]:
         copy.wait_recv()
+    for copy in relayed:
+        copy.wait_recv()
+    for n in range(RING):
+        out_ref[d, :, LANES * n : LANES * n + LANES] = spread_land[n]
 
     def part(n, begin, size):
         return out_ref.at[n, pl.ds(begin, size)]
@@ -437,11 +444,12 @@
             pltpu.VMEM((RING, 4, 432, LANES), BF),
             pltpu.VMEM((RING, 2, 512, LANES), BF),
             pltpu.VMEM((2, 432, LANES), F32),
-            pltpu.VMEM((RING, 2, 432, LANES), BF),
-            pltpu.VMEM((RING, 2, 432, LANES), BF),
+            pltpu.VMEM((RING, 896, LANES), BF),
             pltpu.VMEM((LANES, 512), F32),
             pltpu.VMEM((2, 432, LANES), F32),
-            pltpu.VMEM((2, RING, 128, 432), BF),
+            pltpu.VMEM((896, LANES), BF),
+            pltpu.VMEM((RING, 128, 384), BF),
+            pltpu.VMEM((RING, 128, 512), BF),
             pltpu.VMEM((6, 2, 64, 640), BF),
             pltpu.VMEM((6, 2, 64, 640), BF),
             pltpu.VMEM((2, 2, 64, 640), F32),
@@ -456,6 +464,8 @@
             pltpu.VMEM((4, 128, 384), BF),
             pltpu.VMEM((4, 128, 384), BF),
             pltpu.VMEM((RING, 128, LANES), BF),
+            pltpu.VMEM((RING, 128, LANES), BF),
+            pltpu.VMEM((2, 128, LANES), BF),
             pltpu.SemaphoreType.DMA((3,)),
             pltpu.SemaphoreType.DMA((copies,)),
             pltpu.SemaphoreType.DMA((copies,)),

time: 114 us -> 118 us (1.035)
  Pallas kernels: 108 us -> 112 us
    pallas_call x1, Pallas kernels: 108 us -> 112 us  [on_device(): pl.pallas_call(gather_kernel, out_shape=jax.ShapeDtypeStruct((RING, 128,...]
where the time goes in v3:
time: 118 us
  Pallas kernels  112 us (95%)
  other arithmetic  3.38 us (3%)
  local copies, waits for them, and re-layouts  1.99 us (2%)
    pallas_call x1, Pallas kernels, on_device(): pl.pallas_call(gather_kernel, out_shape=jax.ShapeDtypeStruct((RING, 128,...  112 us
    convert_element_type x1, other arithmetic, on_device(): return gram.reshape(1024, 1024).astype(F32)  2.61 us

profile of v3, /device:TPU:1, one launch (start us, length us, event | category | flops | bytes accessed | tf_op | source)
XLA Modules:
  0.0 117.6 jit_solution(5256531717404495882)
XLA Ops:
  0.7 0.8 fusion.weight_ref
  1.4 1.0 copy.6.slabs_ref
  2.4 0.0 copy-start
  2.4 1.0 copy-done
  3.4 111.6 %shard_map.55 = bf16[8,128,1024]{2,1,0:T(8,128)(2,1)S(1)} custom-call(bf16[2,500,128]{2,1,0:T(8,128)(2,1)S(1)} %copy.6.slabs_ref, bf16[432,500]{1,0:T(8,128)(2,1)S(1)} %bitcast.5, f32[2,432]{1,0:T(2,128)S(1)} %fusion.weight_ref), custom_call_target="tpu_custom_call" | custom-call | flops 2700000000 | bytes 3000000 | tf_op jit(solution)/shard_map/pallas_call | solution.py:435
  115.0 2.6 %bitcast_convert_fusion = f32[1024,1024]{1,0:T(8,128)} fusion(bf16[8,128,1024]{2,1,0:T(8,128)(2,1)S(1)} %shard_map.55), kind=kLoop, calls=%fused_computation | loop fusion | flops 1048576 | bytes 6291456 | tf_op jit(solution)/shard_map/convert_element_type | solution.py:478
Async XLA Ops:
  2.4 1.0 copy-start

commit v4 on v2

--- a/solution.py
+++ b/solution.py
@@ -52,7 +52,7 @@
     slabs_ref, virt_ref, weight_ref, out_ref,
     slab_in, virt_in, weight_in, vq, hs, acc, rp, qp, wrow, wcol, wl,
     a_raw, a_land, a_keep, a_own, a_sib, a_last,
-    b_terms, b_raw, b_land, b_keep, b_own, b_give, b_take, red,
+    b_raw, b_land, b_keep, b_own, b_sib, b_last, red,
     local_sems, send_sems, recv_sems,
 ):
     d, r, c = lax.axis_index("depth"), lax.axis_index("row"), lax.axis_index("col")
@@ -339,16 +339,9 @@
     y_down[3, 1].wait_recv()
     y_up[4, 1].wait_recv()
     y_down[4, 0].wait_recv()
-    b_pair = {}
-    for at, name in enumerate(targets):
-        b_terms[at] = terms_of(name, slots_b)
-        b_give[at] = b_terms[at, 1 - plane].astype(BF)
-        b_pair[name] = send(b_give.at[at], b_take.at[at], depth=d_sib)
-        if at == 0:
-            ring_a.pass_on()
-    for at, name in enumerate(targets):
-        b_pair[name].wait_recv()
-        ring_b.give(name, (b_terms[at, plane] + b_take[at].astype(F32))[None])
+    ring_a.pass_on()
+    for name in targets:
+        ring_b.give(name, terms_of(name, slots_b))
     ring_a.end()
     a_sib[...] = a_own[1 - plane].astype(BF)
     last = send(a_sib, a_last, depth=d_sib)
@@ -374,8 +367,12 @@
         spread.append((to, copy))
         pl.when(in_first(to))(copy.start)
     ring_b.end()
+    b_sib[...] = b_own[1 - plane].astype(BF)
+    last = send(b_sib, b_last, depth=d_sib)
+    last.wait_recv()
+    total = (b_own[plane] + b_last[...].astype(F32)).astype(BF)
     for at, slot in enumerate(slots_b):
-        red[rows_of[slot]] = b_own[0, :, LANES * at : LANES * at + LANES].astype(BF)
+        red[rows_of[slot]] = total[:, LANES * at : LANES * at + LANES]
     for to, copy in spread:
         pl.when(jnp.logical_not(in_first(to)))(copy.start)
     out_ref[d, :, tile(c)] = red[c]
@@ -388,33 +385,33 @@
     def pass_on(n, begin, size, **target):
         return send(part(n, begin, size), part(n, begin, size), **target)
 
-    pair = pass_on(d, 0, 64, depth=d_sib)
-    b_up = pass_on(d, 64, 64, depth=d_up)
-    b_down = pass_on(d, 64, 64, depth=d_down)
-    b_pairs = [pass_on(d, 64, 64, depth=d_sib)]
-    a_up = pass_on(d, 0, 64, depth=d_up)
-    a_down = pass_on(d, 0, 64, depth=d_down)
+    pair = pass_on(d, 0, 96, depth=d_sib)
+    b_up = pass_on(d, 96, 32, depth=d_up)
+    b_down = pass_on(d, 96, 32, depth=d_down)
+    b_pairs = [pass_on(d, 96, 32, depth=d_sib)]
+    a_up = pass_on(d, 0, 96, depth=d_up)
+    a_down = pass_on(d, 0, 96, depth=d_down)
     pair.wait_recv()
-    a_up2 = pass_on(d_sib, 0, 64, depth=d_up)
-    a_down2 = pass_on(d_sib, 0, 64, depth=d_down)
+    a_up2 = pass_on(d_sib, 0, 96, depth=d_up)
+    a_down2 = pass_on(d_sib, 0, 96, depth=d_down)
     b_up.wait_recv()
-    b_up2 = pass_on(d_down, 96, 32, depth=d_up)
-    b_pairs.append(pass_on(d_down, 64, 64, depth=d_sib))
+    b_up2 = pass_on(d_down, 112, 16, depth=d_up)
+    b_pairs.append(pass_on(d_down, 96, 32, depth=d_sib))
     b_down.wait_recv()
-    b_down2 = pass_on(d_up, 64, 32, depth=d_down)
-    b_pairs.append(pass_on(d_up, 64, 64, depth=d_sib))
+    b_down2 = pass_on(d_up, 96, 16, depth=d_down)
+    b_pairs.append(pass_on(d_up, 96, 32, depth=d_sib))
     a_up.wait_recv()
-    a_up3 = pass_on(d_down, 32, 32, depth=d_up)
+    a_up3 = pass_on(d_down, 48, 48, depth=d_up)
     a_down.wait_recv()
-    a_down3 = pass_on(d_up, 0, 32, depth=d_down)
+    a_down3 = pass_on(d_up, 0, 48, depth=d_down)
     b_up2.wait_recv()
-    b_pairs.append(pass_on(d_far, 96, 32, depth=d_sib))
+    b_pairs.append(pass_on(d_far, 112, 16, depth=d_sib))
     b_down2.wait_recv()
-    b_pairs.append(pass_on(d_far, 64, 32, depth=d_sib))
+    b_pairs.append(pass_on(d_far, 96, 16, depth=d_sib))
     a_up2.wait_recv()
-    a_up4 = pass_on(other(d_down), 32, 32, depth=d_up)
+    a_up4 = pass_on(other(d_down), 48, 48, depth=d_up)
     a_down2.wait_recv()
-    a_down4 = pass_on(other(d_up), 0, 32, depth=d_down)
+    a_down4 = pass_on(other(d_up), 0, 48, depth=d_down)
     for copy in (a_up3, a_down3, a_up4, a_down4, *b_pairs):
         copy.wait_recv()
     links.finish()
@@ -448,13 +445,12 @@
             pltpu.VMEM((2, 128, 640), F32),
             pltpu.VMEM((128, 640), BF),
             pltpu.VMEM((128, 640), BF),
-            pltpu.VMEM((4, 2, 128, 384), F32),
-            pltpu.VMEM((6, 1, 64, 384), BF),
-            pltpu.VMEM((6, 1, 64, 384), BF),
-            pltpu.VMEM((2, 1, 64, 384), F32),
-            pltpu.VMEM((1, 128, 384), F32),
-            pltpu.VMEM((4, 128, 384), BF),
-            pltpu.VMEM((4, 128, 384), BF),
+            pltpu.VMEM((6, 2, 64, 384), BF),
+            pltpu.VMEM((6, 2, 64, 384), BF),
+            pltpu.VMEM((2, 2, 64, 384), F32),
+            pltpu.VMEM((2, 128, 384), F32),
+            pltpu.VMEM((128, 384), BF),
+            pltpu.VMEM((128, 384), BF),
             pltpu.VMEM((RING, 128, LANES), BF),
             pltpu.SemaphoreType.DMA((3,)),
             pltpu.SemaphoreType.DMA((copies,)),

time: 114 us -> 119 us (1.044)
  the two profiles are of different devices: /device:TPU:1 before, /device:TPU:40 now
where the time goes in v4:
time: 119 us
  Pallas kernels  113 us (95%)
  other arithmetic  3.38 us (3%)
  local copies, waits for them, and re-layouts  1.99 us (2%)
    pallas_call x1, Pallas kernels, on_device(): pl.pallas_call(gather_kernel, out_shape=jax.ShapeDtypeStruct((RING, 128,...  113 us
    convert_element_type x1, other arithmetic, on_device(): return gram.reshape(1024, 1024).astype(F32)  2.61 us

profile of v4, /device:TPU:40, one launch (start us, length us, event | category | flops | bytes accessed | tf_op | source)
XLA Modules:
  0.0 118.7 jit_solution(7539674852641232917)
XLA Ops:
  0.7 0.8 fusion.weight_ref
  1.4 1.0 copy.6.slabs_ref
  2.4 0.0 copy-start
  2.4 1.0 copy-done
  3.4 112.6 %shard_map.55 = bf16[8,128,1024]{2,1,0:T(8,128)(2,1)S(1)} custom-call(bf16[2,500,128]{2,1,0:T(8,128)(2,1)S(1)} %copy.6.slabs_ref, bf16[432,500]{1,0:T(8,128)(2,1)S(1)} %bitcast.5, f32[2,432]{1,0:T(2,128)S(1)} %fusion.weight_ref), custom_call_target="tpu_custom_call" | custom-call | flops 2700000000 | bytes 3000000 | tf_op jit(solution)/shard_map/pallas_call | solution.py:425
  116.0 2.6 %bitcast_convert_fusion = f32[1024,1024]{1,0:T(8,128)} fusion(bf16[8,128,1024]{2,1,0:T(8,128)(2,1)S(1)} %shard_map.55), kind=kLoop, calls=%fused_computation | loop fusion | flops 1048576 | bytes 6291456 | tf_op jit(solution)/shard_map/convert_element_type | solution.py:464
Async XLA Ops:
  2.4 1.0 copy-start

commit v5 on v2

--- a/solution.py
+++ b/solution.py
@@ -13,8 +13,13 @@
 
 
 class Links:
-    def __init__(self, send_sems, recv_sems):
-        self.send_sems, self.recv_sems, self.copies = send_sems, recv_sems, []
+    def __init__(self, here, send_sems, recv_sems):
+        self.here, self.send_sems, self.recv_sems = here, send_sems, recv_sems
+        self.copies, self.retired = [], 0
+
+    def place(self, **target):
+        at = {**self.here, **target}
+        return at["depth"], at["row"], at["col"]
 
     def plan(self, src, dst, **target):
         at = len(self.copies)
@@ -23,7 +28,7 @@
             dst_ref=dst,
             send_sem=self.send_sems.at[at],
             recv_sem=self.recv_sems.at[at],
-            device_id=target,
+            device_id=self.place(**target),
             device_id_type=MESH,
         )
         self.copies.append(copy)
@@ -34,9 +39,10 @@
         copy.start()
         return copy
 
-    def finish(self):
-        for copy in self.copies:
+    def retire(self, upto=None):
+        for copy in self.copies[self.retired : upto]:
             copy.wait_send()
+        self.retired = len(self.copies) if upto is None else upto
 
 
 def around(me):
@@ -59,7 +65,7 @@
     d_up, d_down, d_far, d_sib = around(d)
     c_up, c_down, c_far, c_sib = around(c)
     r_up, r_down = lax.rem(r + 1, RING), lax.rem(r + 7, RING)
-    links = Links(send_sems, recv_sems)
+    links = Links({"depth": d, "row": r, "col": c}, send_sems, recv_sems)
     send = links.send
 
     loads = [
@@ -69,8 +75,10 @@
     for load in loads:
         load.start()
     barrier = pltpu.get_barrier_semaphore()
-    partners = [{"depth": d_up}, {"depth": d_down}, {"depth": d_sib}, {"row": r_up}, {"row": r_down}]
-    partners += [{"col": lax.rem(c + step, RING)} for step in range(1, RING)]
+    c_far_sib, c_up_sib, c_down_sib = other(c_far), other(c_up), other(c_down)
+    partners = [links.place(depth=to) for to in (d_up, d_down, d_sib)]
+    partners += [links.place(row=to) for to in (r_up, r_down)]
+    partners += [links.place(col=to) for to in (c_up, c_down, c_far, c_sib, c_up_sib, c_down_sib, c_far_sib)]
     for partner in partners:
         pl.semaphore_signal(barrier, inc=1, device_id=partner, device_id_type=MESH)
 
@@ -249,17 +257,20 @@
         couple(n, 1)
 
     panels_out(1)
+    first_stage = len(links.copies)
     y_step(1, 0)
     z_step(0)
     weigh(c, 0)
     weigh(c, 1)
     y_step(1, 1)
+    links.retire(24)
     z_step(1)
     share_own[0].wait_recv()
     weigh(c_sib, 0)
     weigh(c_down, 0)
     y_step(2, 0)
     weigh(c_up, 0)
+    links.retire(40)
     z_down["far"].wait_recv()
     share_far[0] = panel(c_far, 0, col=c_sib)
     share_own[1].wait_recv()
@@ -346,6 +357,7 @@
         b_pair[name] = send(b_give.at[at], b_take.at[at], depth=d_sib)
         if at == 0:
             ring_a.pass_on()
+    links.retire(first_stage)
     for at, name in enumerate(targets):
         b_pair[name].wait_recv()
         ring_b.give(name, (b_terms[at, plane] + b_take[at].astype(F32))[None])
@@ -363,13 +375,13 @@
         apart = lax.rem(at - r + RING, RING)
         return jnp.logical_or(apart <= 2, apart >= 6)
 
+    links.retire(len(links.copies) - 4)
     last.wait_recv()
     total = (a_own[plane] + a_last[...].astype(F32)).astype(BF)
     for at, slot in enumerate(slots_a):
         red[rows_of[slot]] = total[:, LANES * at : LANES * at + LANES]
     spread = []
-    for step in (4, 2, 6, 3, 5, 1, 7):
-        to = lax.rem(c + step, RING)
+    for to in (c_far, c_far_sib, c_up, c_down, c_up_sib, c_down_sib, c_sib):
         copy = links.plan(red.at[to], out_ref.at[d, :, tile(c)], col=to)
         spread.append((to, copy))
         pl.when(in_first(to))(copy.start)
@@ -379,6 +391,7 @@
     for to, copy in spread:
         pl.when(jnp.logical_not(in_first(to)))(copy.start)
     out_ref[d, :, tile(c)] = red[c]
+    links.retire(len(links.copies) - 7)
     for _, copy in spread:
         copy.wait_recv()
 
@@ -394,6 +407,7 @@
     b_pairs = [pass_on(d, 64, 64, depth=d_sib)]
     a_up = pass_on(d, 0, 64, depth=d_up)
     a_down = pass_on(d, 0, 64, depth=d_down)
+    links.retire(len(links.copies) - 6)
     pair.wait_recv()
     a_up2 = pass_on(d_sib, 0, 64, depth=d_up)
     a_down2 = pass_on(d_sib, 0, 64, depth=d_down)
@@ -415,9 +429,10 @@
     a_up4 = pass_on(other(d_down), 32, 32, depth=d_up)
     a_down2.wait_recv()
     a_down4 = pass_on(other(d_up), 0, 32, depth=d_down)
+    links.retire(len(links.copies) - 6)
     for copy in (a_up3, a_down3, a_up4, a_down4, *b_pairs):
         copy.wait_recv()
-    links.finish()
+    links.retire()
 
 
 def on_device(half_slabs, virtuals, occupied_energy, virtual_energy, frequency):

time: 114 us -> 113 us (level)
  Pallas kernels: 108 us -> 106 us
    pallas_call x1, Pallas kernels: 108 us -> 106 us  [on_device(): pl.pallas_call(gather_kernel, out_shape=jax.ShapeDtypeStruct((RING, 128,...]
where the time goes in v5:
time: 113 us; the launch traced here: 112 us
  Pallas kernels  106 us (94%)
  other arithmetic  3.38 us (3%)
  local copies, waits for them, and re-layouts  1.99 us (2%)
    pallas_call x1, Pallas kernels, on_device(): pl.pallas_call(gather_kernel, out_shape=jax.ShapeDtypeStruct((RING, 128,...  106 us
    convert_element_type x1, other arithmetic, on_device(): return gram.reshape(1024, 1024).astype(F32)  2.61 us

profile of v5, /device:TPU:1, one launch (start us, length us, event | category | flops | bytes accessed | tf_op | source)
XLA Modules:
  0.0 112.1 jit_solution(17595741264979267643)
XLA Ops:
  0.7 0.8 fusion.weight_ref
  1.4 1.0 copy.6.slabs_ref
  2.4 0.0 copy-start
  2.4 1.0 copy-done
  3.4 106.0 %shard_map.55 = bf16[8,128,1024]{2,1,0:T(8,128)(2,1)S(1)} custom-call(bf16[2,500,128]{2,1,0:T(8,128)(2,1)S(1)} %copy.6.slabs_ref, bf16[432,500]{1,0:T(8,128)(2,1)S(1)} %bitcast.5, f32[2,432]{1,0:T(2,128)S(1)} %fusion.weight_ref), custom_call_target="tpu_custom_call" | custom-call | flops 2700000000 | bytes 3000000 | tf_op jit(solution)/shard_map/pallas_call | solution.py:443
  109.5 2.6 %bitcast_convert_fusion = f32[1024,1024]{1,0:T(8,128)} fusion(bf16[8,128,1024]{2,1,0:T(8,128)(2,1)S(1)} %shard_map.55), kind=kLoop, calls=%fused_computation | loop fusion | flops 1048576 | bytes 6291456 | tf_op jit(solution)/shard_map/convert_element_type | solution.py:483
Async XLA Ops:
  2.4 1.0 copy-start

commit v6 on v5

--- a/solution.py
+++ b/solution.py
@@ -21,13 +21,13 @@
         at = {**self.here, **target}
         return at["depth"], at["row"], at["col"]
 
-    def plan(self, src, dst, **target):
+    def plan(self, src, dst, recv_sem=None, **target):
         at = len(self.copies)
         copy = pltpu.make_async_remote_copy(
             src_ref=src,
             dst_ref=dst,
             send_sem=self.send_sems.at[at],
-            recv_sem=self.recv_sems.at[at],
+            recv_sem=self.recv_sems.at[at] if recv_sem is None else recv_sem,
             device_id=self.place(**target),
             device_id_type=MESH,
         )
@@ -56,10 +56,10 @@
 
 def gather_kernel(
     slabs_ref, virt_ref, weight_ref, out_ref,
-    slab_in, virt_in, weight_in, vq, hs, acc, rp, qp, wrow, wcol, wl,
+    vq, hs, acc, rp, qp, wrow, wcol, wl,
     a_raw, a_land, a_keep, a_own, a_sib, a_last,
-    b_terms, b_raw, b_land, b_keep, b_own, b_give, b_take, red,
-    local_sems, send_sems, recv_sems,
+    b_terms, b_raw, b_land, b_keep, b_own, b_give, b_take, red, tile_land, parts,
+    send_sems, recv_sems, tile_sems,
 ):
     d, r, c = lax.axis_index("depth"), lax.axis_index("row"), lax.axis_index("col")
     d_up, d_down, d_far, d_sib = around(d)
@@ -68,12 +68,6 @@
     links = Links({"depth": d, "row": r, "col": c}, send_sems, recv_sems)
     send = links.send
 
-    loads = [
-        pltpu.make_async_copy(src, dst, local_sems.at[at])
-        for at, (src, dst) in enumerate(((virt_ref, virt_in), (slabs_ref, slab_in), (weight_ref, weight_in)))
-    ]
-    for load in loads:
-        load.start()
     barrier = pltpu.get_barrier_semaphore()
     c_far_sib, c_up_sib, c_down_sib = other(c_far), other(c_up), other(c_down)
     partners = [links.place(depth=to) for to in (d_up, d_down, d_sib)]
@@ -81,19 +75,24 @@
     partners += [links.place(col=to) for to in (c_up, c_down, c_far, c_sib, c_up_sib, c_down_sib, c_far_sib)]
     for partner in partners:
         pl.semaphore_signal(barrier, inc=1, device_id=partner, device_id_type=MESH)
+    apart = lax.rem(c - r + RING, RING)
+    turned = jnp.logical_or(jnp.logical_or(apart == 3, apart == 6), apart == 7)
+
+    @pl.when(turned)
+    def _():
+        for n in range(RING):
+            pl.semaphore_signal(barrier, inc=1, device_id=links.place(row=c, col=n), device_id_type=MESH)
 
     nvir, nbas = virt_ref.shape
     vq[c, 3] = jnp.zeros((nvir, LANES), BF)
-    for load in loads:
-        load.wait()
     for quarter in range(3):
-        vq[c, quarter] = virt_in[:, LANES * quarter : LANES * quarter + LANES]
-    vq[c, 3, :, 0 : nbas - 384] = virt_in[:, 384:nbas]
+        vq[c, quarter] = virt_ref[:, LANES * quarter : LANES * quarter + LANES]
+    vq[c, 3, :, 0 : nbas - 384] = virt_ref[:, 384:nbas]
     for orbital in range(2):
         hs[d, orbital, 496:512, :] = jnp.zeros((16, LANES), BF)
-        hs[d, orbital, 0:nbas, :] = slab_in[orbital]
-
-    pl.semaphore_wait(barrier, len(partners))
+        hs[d, orbital, 0:nbas, :] = slabs_ref[orbital]
+
+    pl.semaphore_wait(barrier, len(partners) + 3)
 
     j = lax.rem(r, 4)
     j_up, j_down = lax.rem(j + 1, 4), lax.rem(j + 3, 4)
@@ -182,7 +181,7 @@
 
     wrow[...] = jnp.zeros_like(wrow)
     for orbital in range(2):
-        wrow[:, 0:nvir] = jnp.broadcast_to(weight_in[orbital : orbital + 1, :], (LANES, nvir))
+        wrow[:, 0:nvir] = jnp.broadcast_to(weight_ref[orbital : orbital + 1, :], (LANES, nvir))
         wcol[orbital] = wrow[...].T[0:nvir, :]
     acc[...] = jnp.zeros_like(acc)
 
@@ -233,6 +232,8 @@
         y_up[step, o].wait_recv()
         y_up[step + 1, o] = send(qp.at[slot, o], qp.at[slot + 2, o], row=r_up)
         y_down[step, o].wait_recv()
+        if step == 2 and o == 1:
+            return
         y_down[step + 1, o] = send(qp.at[slot + 1, o], qp.at[slot + 3, o], row=r_down)
 
     def z_step(o):
@@ -341,22 +342,20 @@
             self.own[:, high] = self.own[:, high] + land[3].astype(F32) + land[4].astype(F32)
 
     plane = lax.rem(d, 2)
-    slots_a, slots_b = (0, 1, 2, 3, 4), (5, 6, 7)
+    slots_a, slots_b = (5, 7), (0, 2, 4)
     ring_a = RingSum(a_raw, a_land, a_keep, a_own)
     ring_b = RingSum(b_raw, b_land, b_keep, b_own)
-    for name in targets:
-        ring_a.give(name, terms_of(name, slots_a))
-    y_up[3, 0].wait_recv()
-    y_down[3, 1].wait_recv()
-    y_up[4, 1].wait_recv()
-    y_down[4, 0].wait_recv()
     b_pair = {}
     for at, name in enumerate(targets):
         b_terms[at] = terms_of(name, slots_b)
         b_give[at] = b_terms[at, 1 - plane].astype(BF)
         b_pair[name] = send(b_give.at[at], b_take.at[at], depth=d_sib)
-        if at == 0:
-            ring_a.pass_on()
+    y_up[3, 0].wait_recv()
+    y_up[4, 1].wait_recv()
+    y_down[4, 0].wait_recv()
+    for name in targets:
+        ring_a.give(name, terms_of(name, slots_a))
+    ring_a.pass_on()
     links.retire(first_stage)
     for at, name in enumerate(targets):
         b_pair[name].wait_recv()
@@ -366,89 +365,136 @@
     last = send(a_sib, a_last, depth=d_sib)
     ring_b.pass_on()
 
-    rows_of = [r, r_down, r_up, *(lax.rem(r + step, RING) for step in (6, 2, 5, 3, 4))]
-
-    def tile(at):
-        return pl.ds(pl.multiple_of(at * LANES, LANES), LANES)
-
-    def in_first(at):
-        apart = lax.rem(at - r + RING, RING)
-        return jnp.logical_or(apart <= 2, apart >= 6)
-
-    links.retire(len(links.copies) - 4)
+    rows_of = {0: r, 2: r_up, 4: lax.rem(r + 2, RING), 5: lax.rem(r + 5, RING), 7: lax.rem(r + 4, RING)}
+    mine = tile_sems.at[c]
+
+    def tiles_out(slots, total):
+        for at, slot in enumerate(slots):
+            red[slot] = total[:, LANES * at : LANES * at + LANES]
+        for slot in slots:
+            to = rows_of[slot]
+            copy = links.plan(red.at[slot], tile_land.at[c], recv_sem=mine, col=to)
+            straight[slot] = to, copy
+            pl.when(to != c)(copy.start)
+            if slot in (2, 4, 5):
+                links.plan(red.at[slot], tile_land.at[c], recv_sem=mine, row=to, col=r).start()
+
+    straight = {}
     last.wait_recv()
-    total = (a_own[plane] + a_last[...].astype(F32)).astype(BF)
-    for at, slot in enumerate(slots_a):
-        red[rows_of[slot]] = total[:, LANES * at : LANES * at + LANES]
-    spread = []
-    for to in (c_far, c_far_sib, c_up, c_down, c_up_sib, c_down_sib, c_sib):
-        copy = links.plan(red.at[to], out_ref.at[d, :, tile(c)], col=to)
-        spread.append((to, copy))
-        pl.when(in_first(to))(copy.start)
+    tiles_out(slots_a, (a_own[plane] + a_last[...].astype(F32)).astype(BF))
     ring_b.end()
-    for at, slot in enumerate(slots_b):
-        red[rows_of[slot]] = b_own[0, :, LANES * at : LANES * at + LANES].astype(BF)
-    for to, copy in spread:
-        pl.when(jnp.logical_not(in_first(to)))(copy.start)
-    out_ref[d, :, tile(c)] = red[c]
-    links.retire(len(links.copies) - 7)
-    for _, copy in spread:
+    tiles_out(slots_b, b_own[0].astype(BF))
+
+    before = len(links.copies) - 8
+    links.retire(before)
+    for slot, (to, _) in straight.items():
+
+        @pl.when(to == c)
+        def _(slot=slot):
+            tile_land[c] = red[slot]
+
+    for n in range(RING):
+
+        @pl.when(jnp.logical_or(turned, c != n))
+        def _(n=n):
+            pltpu.make_async_remote_copy(
+                src_ref=red.at[0],
+                dst_ref=tile_land.at[n],
+                send_sem=send_sems.at[before],
+                recv_sem=tile_sems.at[n],
+                device_id=links.place(col=c_sib),
+                device_id_type=MESH,
+            ).wait_recv()
+
+    @pl.when(turned)
+    def _():
+        for n in range(RING):
+            parts[d, n] = tile_land[n].T
+
+    @pl.when(jnp.logical_not(turned))
+    def _():
+        parts[d] = tile_land[...]
+
+    def pass_on(n, begin, size, **target):
+        piece = parts.at[n, pl.ds(begin, size)]
+        return send(piece, piece, **target)
+
+    def settle(n):
+        @pl.when(turned)
+        def _():
+            at = pl.ds(pl.multiple_of(LANES * n, LANES), LANES)
+            for m in range(RING):
+                out_ref[m, :, at] = parts[n, m]
+
+        @pl.when(jnp.logical_not(turned))
+        def _():
+            for m in range(RING):
+                out_ref[n, :, LANES * m : LANES * m + LANES] = parts[n, m]
+
+    first_gather = len(links.copies)
+    pair = pass_on(d, 0, 4, depth=d_sib)
+    b_up = pass_on(d, 4, 4, depth=d_up)
+    b_down = pass_on(d, 4, 4, depth=d_down)
+    b_pairs = [pass_on(d, 4, 4, depth=d_sib)]
+    a_up = pass_on(d, 0, 4, depth=d_up)
+    a_down = pass_on(d, 0, 4, depth=d_down)
+    for slot, (to, copy) in straight.items():
+        pl.when(to != c)(copy.wait_send)
+    for at in range(before, first_gather):
+        if all(links.copies[at] is not copy for _, copy in straight.values()):
+            links.copies[at].wait_send()
+    links.retired = first_gather
+    settle(d)
+    pair.wait_recv()
+    a_up2 = pass_on(d_sib, 0, 4, depth=d_up)
+    a_down2 = pass_on(d_sib, 0, 4, depth=d_down)
+    b_up.wait_recv()
+    b_up2 = pass_on(d_down, 6, 2, depth=d_up)
+    b_pairs.append(pass_on(d_down, 4, 4, depth=d_sib))
+    b_down.wait_recv()
+    b_down2 = pass_on(d_up, 4, 2, depth=d_down)
+    b_pairs.append(pass_on(d_up, 4, 4, depth=d_sib))
+    a_up.wait_recv()
+    a_up3 = pass_on(d_down, 2, 2, depth=d_up)
+    a_down.wait_recv()
+    a_down3 = pass_on(d_up, 0, 2, depth=d_down)
+    settle(d_up)
+    settle(d_down)
+    b_up2.wait_recv()
+    b_pairs.append(pass_on(d_far, 6, 2, depth=d_sib))
+    b_down2.wait_recv()
+    b_pairs.append(pass_on(d_far, 4, 2, depth=d_sib))
+    a_up2.wait_recv()
+    a_up4 = pass_on(other(d_down), 2, 2, depth=d_up)
+    a_down2.wait_recv()
+    a_down4 = pass_on(other(d_up), 0, 2, depth=d_down)
+    links.retire(len(links.copies) - 6)
+    b_pairs[0].wait_recv()
+    settle(d_sib)
+    a_up3.wait_recv()
+    a_down3.wait_recv()
+    settle(d_far)
+    b_pairs[1].wait_recv()
+    settle(other(d_down))
+    b_pairs[2].wait_recv()
+    settle(other(d_up))
+    for copy in (a_up4, a_down4, *b_pairs[3:]):
         copy.wait_recv()
-
-    def part(n, begin, size):
-        return out_ref.at[n, pl.ds(begin, size)]
-
-    def pass_on(n, begin, size, **target):
-        return send(part(n, begin, size), part(n, begin, size), **target)
-
-    pair = pass_on(d, 0, 64, depth=d_sib)
-    b_up = pass_on(d, 64, 64, depth=d_up)
-    b_down = pass_on(d, 64, 64, depth=d_down)
-    b_pairs = [pass_on(d, 64, 64, depth=d_sib)]
-    a_up = pass_on(d, 0, 64, depth=d_up)
-    a_down = pass_on(d, 0, 64, depth=d_down)
-    links.retire(len(links.copies) - 6)
-    pair.wait_recv()
-    a_up2 = pass_on(d_sib, 0, 64, depth=d_up)
-    a_down2 = pass_on(d_sib, 0, 64, depth=d_down)
-    b_up.wait_recv()
-    b_up2 = pass_on(d_down, 96, 32, depth=d_up)
-    b_pairs.append(pass_on(d_down, 64, 64, depth=d_sib))
-    b_down.wait_recv()
-    b_down2 = pass_on(d_up, 64, 32, depth=d_down)
-    b_pairs.append(pass_on(d_up, 64, 64, depth=d_sib))
-    a_up.wait_recv()
-    a_up3 = pass_on(d_down, 32, 32, depth=d_up)
-    a_down.wait_recv()
-    a_down3 = pass_on(d_up, 0, 32, depth=d_down)
-    b_up2.wait_recv()
-    b_pairs.append(pass_on(d_far, 96, 32, depth=d_sib))
-    b_down2.wait_recv()
-    b_pairs.append(pass_on(d_far, 64, 32, depth=d_sib))
-    a_up2.wait_recv()
-    a_up4 = pass_on(other(d_down), 32, 32, depth=d_up)
-    a_down2.wait_recv()
-    a_down4 = pass_on(other(d_up), 0, 32, depth=d_down)
-    links.retire(len(links.copies) - 6)
-    for copy in (a_up3, a_down3, a_up4, a_down4, *b_pairs):
-        copy.wait_recv()
+    settle(other(d_far))
     links.retire()
 
 
 def on_device(half_slabs, virtuals, occupied_energy, virtual_energy, frequency):
-    hbm = pl.BlockSpec(memory_space=pltpu.HBM)
+    vmem = pl.BlockSpec(memory_space=pltpu.VMEM)
     excitation = virtual_energy[None, :] - occupied_energy[:, None]
     weight = 4.0 * excitation / (excitation * excitation + frequency[0] * frequency[0])
     copies = 128
     gram = pl.pallas_call(
         gather_kernel,
         out_shape=jax.ShapeDtypeStruct((RING, 128, 1024), BF),
-        in_specs=[hbm] * 3,
-        out_specs=pl.BlockSpec(memory_space=pltpu.VMEM),
+        in_specs=[vmem] * 3,
+        out_specs=vmem,
         scratch_shapes=[
-            pltpu.VMEM((2, 500, LANES), BF),
-            pltpu.VMEM((432, 500), BF),
-            pltpu.VMEM((2, 432), F32),
             pltpu.VMEM((RING, 4, 432, LANES), BF),
             pltpu.VMEM((RING, 2, 512, LANES), BF),
             pltpu.VMEM((2, 432, LANES), F32),
@@ -457,12 +503,12 @@
             pltpu.VMEM((LANES, 512), F32),
             pltpu.VMEM((2, 432, LANES), F32),
             pltpu.VMEM((2, RING, 128, 432), BF),
-            pltpu.VMEM((6, 2, 64, 640), BF),
-            pltpu.VMEM((6, 2, 64, 640), BF),
-            pltpu.VMEM((2, 2, 64, 640), F32),
-            pltpu.VMEM((2, 128, 640), F32),
-            pltpu.VMEM((128, 640), BF),
-            pltpu.VMEM((128, 640), BF),
+            pltpu.VMEM((6, 2, 64, 256), BF),
+            pltpu.VMEM((6, 2, 64, 256), BF),
+            pltpu.VMEM((2, 2, 64, 256), F32),
+            pltpu.VMEM((2, 128, 256), F32),
+            pltpu.VMEM((128, 256), BF),
+            pltpu.VMEM((128, 256), BF),
             pltpu.VMEM((4, 2, 128, 384), F32),
             pltpu.VMEM((6, 1, 64, 384), BF),
             pltpu.VMEM((6, 1, 64, 384), BF),
@@ -471,9 +517,11 @@
             pltpu.VMEM((4, 128, 384), BF),
             pltpu.VMEM((4, 128, 384), BF),
             pltpu.VMEM((RING, 128, LANES), BF),
-            pltpu.SemaphoreType.DMA((3,)),
+            pltpu.VMEM((RING, 128, LANES), BF),
+            pltpu.VMEM((RING, RING, 128, LANES), BF),
             pltpu.SemaphoreType.DMA((copies,)),
             pltpu.SemaphoreType.DMA((copies,)),
+            pltpu.SemaphoreType.DMA((RING,)),
         ],
         compiler_params=pltpu.CompilerParams(
             collective_id=0, has_side_effects=True, vmem_limit_bytes=48 * 2**20

time: 113 us -> 110 us (0.973)
  Pallas kernels: 106 us -> 103 us
    pallas_call x1, Pallas kernels: 106 us -> 103 us  [on_device(): pl.pallas_call(gather_kernel, out_shape=jax.ShapeDtypeStruct((RING, 128,...]
where the time goes in v6:
time: 110 us; the launch traced here: 109 us
  Pallas kernels  103 us (94%)
  other arithmetic  3.38 us (3%)
  local copies, waits for them, and re-layouts  1.99 us (2%)
    pallas_call x1, Pallas kernels, on_device(): pl.pallas_call(gather_kernel, out_shape=jax.ShapeDtypeStruct((RING, 128,...  103 us
    convert_element_type x1, other arithmetic, on_device(): return gram.reshape(1024, 1024).astype(F32)  2.61 us

profile of v6, /device:TPU:1, one launch (start us, length us, event | category | flops | bytes accessed | tf_op | source)
XLA Modules:
  0.0 109.3 jit_solution(1307899322114529999)
XLA Ops:
  0.7 0.8 fusion.weight_ref
  1.4 1.0 copy.6.slabs_ref
  2.4 0.0 copy-start
  2.4 1.0 copy-done
  3.4 103.2 %shard_map.55 = bf16[8,128,1024]{2,1,0:T(8,128)(2,1)S(1)} custom-call(bf16[2,500,128]{2,1,0:T(8,128)(2,1)S(1)} %copy.6.slabs_ref, bf16[432,500]{1,0:T(8,128)(2,1)S(1)} %bitcast.5, f32[2,432]{1,0:T(2,128)S(1)} %fusion.weight_ref), custom_call_target="tpu_custom_call" | custom-call | flops 2700000000 | bytes 3000000 | tf_op jit(solution)/shard_map/pallas_call | solution.py:492
  106.7 2.6 %bitcast_convert_fusion = f32[1024,1024]{1,0:T(8,128)} fusion(bf16[8,128,1024]{2,1,0:T(8,128)(2,1)S(1)} %shard_map.55), kind=kLoop, calls=%fused_computation | loop fusion | flops 1048576 | bytes 6291456 | tf_op jit(solution)/shard_map/convert_element_type | solution.py:531
Async XLA Ops:
  2.4 1.0 copy-start

commit v7 on v6

--- a/solution.py
+++ b/solution.py
@@ -102,12 +102,12 @@
         piece = hs.at[n, orbital] if half is None else hs.at[n, orbital, pl.ds(256 * half, 256)]
         return send(piece, piece, **target)
 
-    def virt(n, quarter, half, **target):
-        piece = vq.at[n, quarter, spans[half]]
+    def virt(n, quarter, half=None, **target):
+        piece = vq.at[n, quarter] if half is None else vq.at[n, quarter, spans[half]]
         return send(piece, piece, **target)
 
-    def virt_rows(n, half):
-        return virt(n, j, half, row=r_up), virt(n, j, half, row=r_down)
+    def virt_rows(n):
+        return virt(n, j, row=r_up), virt(n, j, row=r_down)
 
     pair, up, down, up2, down2, up3, down3, up4, down4 = ({} for _ in range(9))
 
@@ -134,48 +134,45 @@
         for copy in (up3[o], down3[o], up4[o], down4[o]):
             copy.wait_recv()
 
-    z_up = {1: virt(c, j, 1, col=c_up)}
-    z_down = {0: virt(c, j, 0, col=c_down)}
-    z_up[0] = virt(c, j, 0, col=c_up)
-    z_down[1] = virt(c, j, 1, col=c_down)
+    z_up = virt(c, j, col=c_up)
+    z_down = virt(c, j, col=c_down)
     slabs_out(0)
     pair[0] = slab(d, 0, depth=d_sib)
     share_own = send(vq.at[c], vq.at[c], col=c_sib)
-
-    rows_a, rows_b, rows_c = {}, {}, {}
-    z_up[1].wait_recv()
+    slabs_out(1)
+
+    z_up.wait_recv()
     z_up2 = virt(c_down, j, 1, col=c_up)
-    rows_a[1] = virt_rows(c_down, 1)
-    z_down[0].wait_recv()
+    rows_a = virt_rows(c_down)
+    z_down.wait_recv()
     z_down2 = virt(c_up, j, 0, col=c_down)
-    rows_b[0] = virt_rows(c_up, 0)
-    z_up[0].wait_recv()
-    rows_a[0] = virt_rows(c_down, 0)
-    z_down[1].wait_recv()
-    rows_b[1] = virt_rows(c_up, 1)
+    rows_b = virt_rows(c_up)
     slabs_sib(0)
     slabs_on(0)
     z_up2.wait_recv()
-    rows_c[1] = virt_rows(c_far, 1)
     z_down2.wait_recv()
-    rows_c[0] = virt_rows(c_far, 0)
+    rows_c = virt_rows(c_far)
     pair[1] = slab(d, 1, depth=d_sib)
-    slabs_out(1)
-
-    def pass_up(n, rows):
-        rows[1][0].wait_recv()
-        return virt(n, j_down, 1, row=r_up)
-
-    def pass_down(n, rows):
-        rows[0][1].wait_recv()
-        return virt(n, j_up, 0, row=r_down)
-
-    on_a = [pass_up(c_down, rows_a)]
-    on_b = [pass_down(c_up, rows_b)]
-    on_a.append(pass_down(c_down, rows_a))
-    on_b.append(pass_up(c_up, rows_b))
+
+    def pass_rows(n, rows):
+        rows[0].wait_recv()
+        if n is c_down:
+            one = (virt(n, j_down, row=r_up),)
+        elif n is c_far:
+            one = (virt(n, j_down, 1, row=r_up),)
+        else:
+            one = ()
+        rows[1].wait_recv()
+        if n is c_up:
+            one += (virt(n, j_up, row=r_down),)
+        elif n is c_far:
+            one += (virt(n, j_up, 0, row=r_down),)
+        return one
+
+    on_a = pass_rows(c_down, rows_a)
+    on_b = pass_rows(c_up, rows_b)
     slabs_sib_on(0)
-    on_c = [pass_up(c_far, rows_c), pass_down(c_far, rows_c)]
+    on_c = pass_rows(c_far, rows_c)
     slabs_sib(1)
     slabs_on(1)
 
@@ -185,8 +182,8 @@
         wcol[orbital] = wrow[...].T[0:nvir, :]
     acc[...] = jnp.zeros_like(acc)
 
-    def virt_end(n, rows, on):
-        for copy in (rows[0][0], rows[1][1], *on):
+    def virt_end(n, on):
+        for copy in on:
             copy.wait_recv()
         return send(vq.at[n], vq.at[n], col=c_sib)
 
@@ -194,15 +191,15 @@
         left = jnp.concatenate([vq[n, 0], vq[n, 1], vq[n, 2], vq[n, 3]], axis=1)
         acc[orbital] += jnp.dot(left, hs[n, orbital], preferred_element_type=F32)
 
-    share_a = virt_end(c_down, rows_a, on_a)
-    share_b = virt_end(c_up, rows_b, on_b)
+    share_a = virt_end(c_down, on_a)
+    share_b = virt_end(c_up, on_b)
     slabs_end(0)
     couple(c, 0)
     share_own.wait_recv()
     couple(c_sib, 0)
     couple(c_down, 0)
     couple(c_up, 0)
-    share_c = virt_end(c_far, rows_c, on_c)
+    share_c = virt_end(c_far, on_c)
     slabs_sib_on(1)
     share_a.wait_recv()
     couple(other(c_down), 0)
@@ -329,10 +326,9 @@
             else:
                 self.own[...] = block
 
-        def pass_on(self):
-            for at, target in ((0, d_up), (1, d_down)):
-                self.copies[at].wait_recv()
-                self.send(at + 4, self.keep[at] + self.land[at].astype(F32), depth=target)
+        def pass_on(self, at):
+            self.copies[at].wait_recv()
+            self.send(at + 4, self.keep[at] + self.land[at].astype(F32), depth=(d_up, d_down)[at])
 
         def end(self):
             for at in (2, 3, 4, 5):
@@ -346,24 +342,14 @@
     ring_a = RingSum(a_raw, a_land, a_keep, a_own)
     ring_b = RingSum(b_raw, b_land, b_keep, b_own)
     b_pair = {}
-    for at, name in enumerate(targets):
+    def gram_b(at, name):
         b_terms[at] = terms_of(name, slots_b)
         b_give[at] = b_terms[at, 1 - plane].astype(BF)
         b_pair[name] = send(b_give.at[at], b_take.at[at], depth=d_sib)
-    y_up[3, 0].wait_recv()
-    y_up[4, 1].wait_recv()
-    y_down[4, 0].wait_recv()
-    for name in targets:
-        ring_a.give(name, terms_of(name, slots_a))
-    ring_a.pass_on()
-    links.retire(first_stage)
-    for at, name in enumerate(targets):
+
+    def pair_b(at, name):
         b_pair[name].wait_recv()
         ring_b.give(name, (b_terms[at, plane] + b_take[at].astype(F32))[None])
-    ring_a.end()
-    a_sib[...] = a_own[1 - plane].astype(BF)
-    last = send(a_sib, a_last, depth=d_sib)
-    ring_b.pass_on()
 
     rows_of = {0: r, 2: r_up, 4: lax.rem(r + 2, RING), 5: lax.rem(r + 5, RING), 7: lax.rem(r + 4, RING)}
     mine = tile_sems.at[c]
@@ -380,10 +366,34 @@
                 links.plan(red.at[slot], tile_land.at[c], recv_sem=mine, row=to, col=r).start()
 
     straight = {}
+
+    gram_b(0, "far")
+    gram_b(1, "up")
+    gram_b(2, "down")
+    y_up[3, 0].wait_recv()
+    y_up[4, 1].wait_recv()
+    y_down[4, 0].wait_recv()
+    ring_a.give("far", terms_of("far", slots_a))
+    ring_a.give("down", terms_of("down", slots_a))
+    pair_b(0, "far")
+    ring_a.give("up", terms_of("up", slots_a))
+    gram_b(3, "own")
+    ring_a.pass_on(1)
+    ring_a.pass_on(0)
+    pair_b(1, "up")
+    pair_b(2, "down")
+    ring_a.give("own", terms_of("own", slots_a))
+    links.retire(first_stage)
+    ring_b.pass_on(0)
+    ring_b.pass_on(1)
+    ring_a.end()
+    a_sib[...] = a_own[1 - plane].astype(BF)
+    last = send(a_sib, a_last, depth=d_sib)
+    pair_b(3, "own")
+    ring_b.end()
+    tiles_out(slots_b, b_own[0].astype(BF))
     last.wait_recv()
     tiles_out(slots_a, (a_own[plane] + a_last[...].astype(F32)).astype(BF))
-    ring_b.end()
-    tiles_out(slots_b, b_own[0].astype(BF))
 
     before = len(links.copies) - 8
     links.retire(before)

time: 110 us -> 107 us (0.973)
  Pallas kernels: 103 us -> 99.4 us
    pallas_call x1, Pallas kernels: 103 us -> 99.4 us  [on_device(): pl.pallas_call(gather_kernel, out_shape=jax.ShapeDtypeStruct((RING, 128,...]
where the time goes in v7:
time: 107 us; the launch traced here: 105 us
  Pallas kernels  99.4 us (93%)
  other arithmetic  3.38 us (3%)
  local copies, waits for them, and re-layouts  1.99 us (2%)
    pallas_call x1, Pallas kernels, on_device(): pl.pallas_call(gather_kernel, out_shape=jax.ShapeDtypeStruct((RING, 128,...  99.4 us
    convert_element_type x1, other arithmetic, on_device(): return gram.reshape(1024, 1024).astype(F32)  2.61 us

profile of v7, /device:TPU:1, one launch (start us, length us, event | category | flops | bytes accessed | tf_op | source)
XLA Modules:
  0.0 105.4 jit_solution(10082843559079899087)
XLA Ops:
  0.7 0.8 fusion.weight_ref
  1.4 1.0 copy.6.slabs_ref
  2.4 0.0 copy-start
  2.4 1.0 copy-done
  3.4 99.4 %shard_map.55 = bf16[8,128,1024]{2,1,0:T(8,128)(2,1)S(1)} custom-call(bf16[2,500,128]{2,1,0:T(8,128)(2,1)S(1)} %copy.6.slabs_ref, bf16[432,500]{1,0:T(8,128)(2,1)S(1)} %bitcast.5, f32[2,432]{1,0:T(2,128)S(1)} %fusion.weight_ref), custom_call_target="tpu_custom_call" | custom-call | flops 2700000000 | bytes 3000000 | tf_op jit(solution)/shard_map/pallas_call | solution.py:502
  102.8 2.6 %bitcast_convert_fusion = f32[1024,1024]{1,0:T(8,128)} fusion(bf16[8,128,1024]{2,1,0:T(8,128)(2,1)S(1)} %shard_map.55), kind=kLoop, calls=%fused_computation | loop fusion | flops 1048576 | bytes 6291456 | tf_op jit(solution)/shard_map/convert_element_type | solution.py:541
Async XLA Ops:
  2.4 1.0 copy-start

commit v8 on v7

--- a/solution.py
+++ b/solution.py
@@ -138,7 +138,7 @@
     z_down = virt(c, j, col=c_down)
     slabs_out(0)
     pair[0] = slab(d, 0, depth=d_sib)
-    share_own = send(vq.at[c], vq.at[c], col=c_sib)
+    share_virt = send(vq.at[c], vq.at[c], col=c_sib)
     slabs_out(1)
 
     z_up.wait_recv()
@@ -195,7 +195,7 @@
     share_b = virt_end(c_up, on_b)
     slabs_end(0)
     couple(c, 0)
-    share_own.wait_recv()
+    share_virt.wait_recv()
     couple(c_sib, 0)
     couple(c_down, 0)
     couple(c_up, 0)
@@ -213,7 +213,10 @@
         return send(rp.at[n, orbital], rp.at[n, orbital], **target)
 
     y_up, y_down, z_up, z_down = {}, {}, {}, {}
-    share_own, share_down, share_up, share_far = {}, {}, {}, {}
+    share = {}
+
+    def whole(n):
+        return send(rp.at[n], rp.at[n], col=c_sib)
 
     def panels_out(o):
         rp[c, o] = acc[o].astype(BF)
@@ -221,7 +224,6 @@
         y_down[1, o] = send(rp.at[c, o], qp.at[2, o], row=r_down)
         z_up[o] = panel(c, o, col=c_up)
         z_down[o] = panel(c, o, col=c_down)
-        share_own[o] = panel(c, o, col=c_sib)
         qp[0, o] = rp[c, o]
 
     def y_step(step, o):
@@ -233,16 +235,6 @@
             return
         y_down[step + 1, o] = send(qp.at[slot + 1, o], qp.at[slot + 3, o], row=r_down)
 
-    def z_step(o):
-        z_up[o].wait_recv()
-        if o == 1:
-            z_up["far"] = panel(c_down, 1, col=c_up)
-        share_down[o] = panel(c_down, o, col=c_sib)
-        z_down[o].wait_recv()
-        if o == 0:
-            z_down["far"] = panel(c_up, 0, col=c_down)
-        share_up[o] = panel(c_up, o, col=c_sib)
-
     def weigh(n, o):
         product = wcol[o] * rp[n, o].astype(F32)
         wl[o, n] = product.astype(BF).T
@@ -256,43 +248,48 @@
 
     panels_out(1)
     first_stage = len(links.copies)
+    y_step(1, 1)
+    z_down[0].wait_recv()
+    z_down["far"] = panel(c_up, 0, col=c_down)
+    share["own"] = whole(c)
     y_step(1, 0)
-    z_step(0)
+    z_up[1].wait_recv()
+    z_up["far"] = panel(c_down, 1, col=c_up)
+    z_up[0].wait_recv()
+    weigh(c, 1)
+    z_down[1].wait_recv()
+    weigh(c_up, 0)
+    weigh(c_down, 0)
+    links.retire(24)
+    links.retire(40)
+    share["down"] = whole(c_down)
+    share["own"].wait_recv()
+    weigh(c_sib, 0)
     weigh(c, 0)
-    weigh(c, 1)
-    y_step(1, 1)
-    links.retire(24)
-    z_step(1)
-    share_own[0].wait_recv()
-    weigh(c_sib, 0)
-    weigh(c_down, 0)
+    y_step(2, 1)
     y_step(2, 0)
-    weigh(c_up, 0)
-    links.retire(40)
+    weigh(c_sib, 1)
     z_down["far"].wait_recv()
-    share_far[0] = panel(c_far, 0, col=c_sib)
-    share_own[1].wait_recv()
-    weigh(c_sib, 1)
-    y_step(2, 1)
     weigh(c_down, 1)
+    share["down"].wait_recv()
+    share["up"] = whole(c_up)
+    weigh(c_down_sib, 1)
+    weigh(c_far, 0)
     z_up["far"].wait_recv()
-    share_far[1] = panel(c_far, 1, col=c_sib)
+    share["far"] = whole(c_far)
+    weigh(c_down_sib, 0)
+    weigh(c_far, 1)
     weigh(c_up, 1)
-    weigh(c_far, 0)
-    for n, share in ((other(c_down), share_down), (other(c_up), share_up)):
-        share[0].wait_recv()
-        weigh(n, 0)
+    y_up[3, 1].wait_recv()
+    y_up[4, 1] = send(qp.at[5, 1], qp.at[7, 1], row=r_up)
     y_down[3, 0].wait_recv()
     y_down[4, 0] = send(qp.at[6, 0], qp.at[7, 0], row=r_down)
-    for n, share in ((other(c_down), share_down), (other(c_up), share_up)):
-        share[1].wait_recv()
-        weigh(n, 1)
-    y_up[3, 1].wait_recv()
-    y_up[4, 1] = send(qp.at[5, 1], qp.at[7, 1], row=r_up)
-    weigh(c_far, 1)
-    for o in range(2):
-        share_far[o].wait_recv()
-        weigh(other(c_far), o)
+    share["up"].wait_recv()
+    weigh(c_up_sib, 0)
+    share["far"].wait_recv()
+    weigh(c_far_sib, 0)
+    weigh(c_up_sib, 1)
+    weigh(c_far_sib, 1)
 
     low, high = slice(0, 64), slice(64, 128)
     targets = {"far": d_far, "up": d_up, "down": d_down, "own": d}

time: 107 us -> 105 us (0.981)
  Pallas kernels: 99.4 us -> 97.4 us
    pallas_call x1, Pallas kernels: 99.4 us -> 97.4 us  [on_device(): pl.pallas_call(gather_kernel, out_shape=jax.ShapeDtypeStruct((RING, 128,...]
where the time goes in v8:
time: 105 us; the launch traced here: 103 us
  Pallas kernels  97.4 us (93%)
  other arithmetic  3.38 us (3%)
  local copies, waits for them, and re-layouts  1.99 us (2%)
    pallas_call x1, Pallas kernels, on_device(): pl.pallas_call(gather_kernel, out_shape=jax.ShapeDtypeStruct((RING, 128,...  97.4 us
    convert_element_type x1, other arithmetic, on_device(): return gram.reshape(1024, 1024).astype(F32)  2.61 us

profile of v8, /device:TPU:1, one launch (start us, length us, event | category | flops | bytes accessed | tf_op | source)
XLA Modules:
  0.0 103.5 jit_solution(18245251262280517900)
XLA Ops:
  0.7 0.8 fusion.weight_ref
  1.4 1.0 copy.6.slabs_ref
  2.4 0.0 copy-start
  2.4 1.0 copy-done
  3.4 97.4 %shard_map.55 = bf16[8,128,1024]{2,1,0:T(8,128)(2,1)S(1)} custom-call(bf16[2,500,128]{2,1,0:T(8,128)(2,1)S(1)} %copy.6.slabs_ref, bf16[432,500]{1,0:T(8,128)(2,1)S(1)} %bitcast.5, f32[2,432]{1,0:T(2,128)S(1)} %fusion.weight_ref), custom_call_target="tpu_custom_call" | custom-call | flops 2700000000 | bytes 3000000 | tf_op jit(solution)/shard_map/pallas_call | solution.py:499
  100.8 2.6 %bitcast_convert_fusion = f32[1024,1024]{1,0:T(8,128)} fusion(bf16[8,128,1024]{2,1,0:T(8,128)(2,1)S(1)} %shard_map.55), kind=kLoop, calls=%fused_computation | loop fusion | flops 1048576 | bytes 6291456 | tf_op jit(solution)/shard_map/convert_element_type | solution.py:538
Async XLA Ops:
  2.4 1.0 copy-start

commit v9 on v8

--- a/solution.py
+++ b/solution.py
@@ -400,51 +400,59 @@
         def _(slot=slot):
             tile_land[c] = red[slot]
 
-    for n in range(RING):
-
-        @pl.when(jnp.logical_or(turned, c != n))
-        def _(n=n):
-            pltpu.make_async_remote_copy(
-                src_ref=red.at[0],
-                dst_ref=tile_land.at[n],
-                send_sem=send_sems.at[before],
-                recv_sem=tile_sems.at[n],
-                device_id=links.place(col=c_sib),
-                device_id_type=MESH,
-            ).wait_recv()
-
-    @pl.when(turned)
-    def _():
-        for n in range(RING):
-            parts[d, n] = tile_land[n].T
-
-    @pl.when(jnp.logical_not(turned))
-    def _():
-        parts[d] = tile_land[...]
+    def columns_of(place):
+        pair_at = lax.rem(c // 2 + place, 4)
+        return [(2 * place + core, 2 * pair_at + core) for core in range(2)]
+
+    def tiles_in(places):
+        for place in places:
+            for at, n in columns_of(place):
+
+                @pl.when(jnp.logical_or(turned, c != n))
+                def _(n=n):
+                    pltpu.make_async_remote_copy(
+                        src_ref=red.at[0],
+                        dst_ref=tile_land.at[n],
+                        send_sem=send_sems.at[before],
+                        recv_sem=tile_sems.at[n],
+                        device_id=links.place(col=c_sib),
+                        device_id_type=MESH,
+                    ).wait_recv()
+
+                @pl.when(turned)
+                def _(at=at, n=n):
+                    parts[d, at] = tile_land[n].T
+
+                @pl.when(jnp.logical_not(turned))
+                def _(at=at, n=n):
+                    parts[d, at] = tile_land[n]
 
     def pass_on(n, begin, size, **target):
         piece = parts.at[n, pl.ds(begin, size)]
         return send(piece, piece, **target)
 
     def settle(n):
+        targets_of = [pair for place in range(4) for pair in columns_of(place)]
+
         @pl.when(turned)
         def _():
-            at = pl.ds(pl.multiple_of(LANES * n, LANES), LANES)
-            for m in range(RING):
-                out_ref[m, :, at] = parts[n, m]
+            for at, m in targets_of:
+                out_ref[m, :, pl.ds(pl.multiple_of(LANES * n, LANES), LANES)] = parts[n, at]
 
         @pl.when(jnp.logical_not(turned))
         def _():
-            for m in range(RING):
-                out_ref[n, :, LANES * m : LANES * m + LANES] = parts[n, m]
+            for at, m in targets_of:
+                out_ref[n, :, pl.ds(pl.multiple_of(LANES * m, LANES), LANES)] = parts[n, at]
 
     first_gather = len(links.copies)
+    tiles_in((0, 1))
     pair = pass_on(d, 0, 4, depth=d_sib)
+    a_up = pass_on(d, 0, 4, depth=d_up)
+    a_down = pass_on(d, 0, 4, depth=d_down)
+    tiles_in((3, 2))
     b_up = pass_on(d, 4, 4, depth=d_up)
     b_down = pass_on(d, 4, 4, depth=d_down)
     b_pairs = [pass_on(d, 4, 4, depth=d_sib)]
-    a_up = pass_on(d, 0, 4, depth=d_up)
-    a_down = pass_on(d, 0, 4, depth=d_down)
     for slot, (to, copy) in straight.items():
         pl.when(to != c)(copy.wait_send)
     for at in range(before, first_gather):

time: 105 us -> 105 us (level); the launches traced: 103 us -> 105 us
  Pallas kernels: 97.4 us -> 98.5 us
    pallas_call x1, Pallas kernels: 97.4 us -> 98.5 us  [on_device(): pl.pallas_call(gather_kernel, out_shape=jax.ShapeDtypeStruct((RING, 128,...]
where the time goes in v9:
time: 105 us
  Pallas kernels  98.5 us (94%)
  other arithmetic  3.38 us (3%)
  local copies, waits for them, and re-layouts  1.99 us (2%)
    pallas_call x1, Pallas kernels, on_device(): pl.pallas_call(gather_kernel, out_shape=jax.ShapeDtypeStruct((RING, 128,...  98.5 us
    convert_element_type x1, other arithmetic, on_device(): return gram.reshape(1024, 1024).astype(F32)  2.61 us

profile of v9, /device:TPU:1, one launch (start us, length us, event | category | flops | bytes accessed | tf_op | source)
XLA Modules:
  0.0 104.6 jit_solution(7675441714859419148)
XLA Ops:
  0.7 0.8 fusion.weight_ref
  1.4 1.0 copy.6.slabs_ref
  2.4 0.0 copy-start
  2.4 1.0 copy-done
  3.4 98.5 %shard_map.55 = bf16[8,128,1024]{2,1,0:T(8,128)(2,1)S(1)} custom-call(bf16[2,500,128]{2,1,0:T(8,128)(2,1)S(1)} %copy.6.slabs_ref, bf16[432,500]{1,0:T(8,128)(2,1)S(1)} %bitcast.5, f32[2,432]{1,0:T(2,128)S(1)} %fusion.weight_ref), custom_call_target="tpu_custom_call" | custom-call | flops 2700000000 | bytes 3000000 | tf_op jit(solution)/shard_map/pallas_call | solution.py:507
  101.9 2.6 %bitcast_convert_fusion = f32[1024,1024]{1,0:T(8,128)} fusion(bf16[8,128,1024]{2,1,0:T(8,128)(2,1)S(1)} %shard_map.55), kind=kLoop, calls=%fused_computation | loop fusion | flops 1048576 | bytes 6291456 | tf_op jit(solution)/shard_map/convert_element_type | solution.py:546
Async XLA Ops:
  2.4 1.0 copy-start

commit v10 on v9

--- a/solution.py
+++ b/solution.py
@@ -342,10 +342,12 @@
     def gram_b(at, name):
         b_terms[at] = terms_of(name, slots_b)
         b_give[at] = b_terms[at, 1 - plane].astype(BF)
-        b_pair[name] = send(b_give.at[at], b_take.at[at], depth=d_sib)
+        if at % 2 == 1:
+            b_pair[at] = send(b_give.at[pl.ds(at - 1, 2)], b_take.at[pl.ds(at - 1, 2)], depth=d_sib)
 
     def pair_b(at, name):
-        b_pair[name].wait_recv()
+        if at % 2 == 0:
+            b_pair[at + 1].wait_recv()
         ring_b.give(name, (b_terms[at, plane] + b_take[at].astype(F32))[None])
 
     rows_of = {0: r, 2: r_up, 4: lax.rem(r + 2, RING), 5: lax.rem(r + 5, RING), 7: lax.rem(r + 4, RING)}
@@ -356,11 +358,13 @@
             red[slot] = total[:, LANES * at : LANES * at + LANES]
         for slot in slots:
             to = rows_of[slot]
+            if slot in (2, 4, 5):
+                links.plan(red.at[slot], tile_land.at[c], recv_sem=mine, row=to, col=r).start()
+        for slot in slots:
+            to = rows_of[slot]
             copy = links.plan(red.at[slot], tile_land.at[c], recv_sem=mine, col=to)
             straight[slot] = to, copy
             pl.when(to != c)(copy.start)
-            if slot in (2, 4, 5):
-                links.plan(red.at[slot], tile_land.at[c], recv_sem=mine, row=to, col=r).start()
 
     straight = {}
 
@@ -372,25 +376,25 @@
     y_down[4, 0].wait_recv()
     ring_a.give("far", terms_of("far", slots_a))
     ring_a.give("down", terms_of("down", slots_a))
-    pair_b(0, "far")
     ring_a.give("up", terms_of("up", slots_a))
     gram_b(3, "own")
+    ring_a.pass_on(0)
+    ring_a.give("own", terms_of("own", slots_a))
     ring_a.pass_on(1)
-    ring_a.pass_on(0)
-    pair_b(1, "up")
-    pair_b(2, "down")
-    ring_a.give("own", terms_of("own", slots_a))
-    links.retire(first_stage)
-    ring_b.pass_on(0)
-    ring_b.pass_on(1)
+    pair_b(0, "far")
     ring_a.end()
     a_sib[...] = a_own[1 - plane].astype(BF)
     last = send(a_sib, a_last, depth=d_sib)
+    pair_b(1, "up")
+    pair_b(2, "down")
+    ring_b.pass_on(0)
     pair_b(3, "own")
+    ring_b.pass_on(1)
+    last.wait_recv()
+    tiles_out(slots_a, (a_own[plane] + a_last[...].astype(F32)).astype(BF))
+    links.retire(first_stage)
     ring_b.end()
     tiles_out(slots_b, b_own[0].astype(BF))
-    last.wait_recv()
-    tiles_out(slots_a, (a_own[plane] + a_last[...].astype(F32)).astype(BF))
 
     before = len(links.copies) - 8
     links.retire(before)

time: 105 us -> 108 us (1.029)
  Pallas kernels: 98.5 us -> 102 us
    pallas_call x1, Pallas kernels: 98.5 us -> 102 us  [on_device(): pl.pallas_call(gather_kernel, out_shape=jax.ShapeDtypeStruct((RING, 128,...]
where the time goes in v10:
time: 108 us
  Pallas kernels  102 us (94%)
  other arithmetic  3.38 us (3%)
  local copies, waits for them, and re-layouts  1.99 us (2%)
    pallas_call x1, Pallas kernels, on_device(): pl.pallas_call(gather_kernel, out_shape=jax.ShapeDtypeStruct((RING, 128,...  102 us
    convert_element_type x1, other arithmetic, on_device(): return gram.reshape(1024, 1024).astype(F32)  2.61 us

profile of v10, /device:TPU:1, one launch (start us, length us, event | category | flops | bytes accessed | tf_op | source)
XLA Modules:
  0.0 108.1 jit_solution(6627582422309838147)
XLA Ops:
  0.7 0.8 fusion.weight_ref
  1.4 1.0 copy.6.slabs_ref
  2.4 0.0 copy-start
  2.4 1.0 copy-done
  3.4 102.0 %shard_map.55 = bf16[8,128,1024]{2,1,0:T(8,128)(2,1)S(1)} custom-call(bf16[2,500,128]{2,1,0:T(8,128)(2,1)S(1)} %copy.6.slabs_ref, bf16[432,500]{1,0:T(8,128)(2,1)S(1)} %bitcast.5, f32[2,432]{1,0:T(2,128)S(1)} %fusion.weight_ref), custom_call_target="tpu_custom_call" | custom-call | flops 2700000000 | bytes 3000000 | tf_op jit(solution)/shard_map/pallas_call | solution.py:511
  105.5 2.6 %bitcast_convert_fusion = f32[1024,1024]{1,0:T(8,128)} fusion(bf16[8,128,1024]{2,1,0:T(8,128)(2,1)S(1)} %shard_map.55), kind=kLoop, calls=%fused_computation | loop fusion | flops 1048576 | bytes 6291456 | tf_op jit(solution)/shard_map/convert_element_type | solution.py:550
Async XLA Ops:
  2.4 1.0 copy-start

commit v11 on v9

--- a/solution.py
+++ b/solution.py
@@ -109,7 +109,7 @@
     def virt_rows(n):
         return virt(n, j, row=r_up), virt(n, j, row=r_down)
 
-    pair, up, down, up2, down2, up3, down3, up4, down4 = ({} for _ in range(9))
+    pair, up, down, up2, down2, up3, down3 = ({} for _ in range(7))
 
     def slabs_out(o):
         up[o], down[o] = slab(d, o, depth=d_up), slab(d, o, depth=d_down)
@@ -118,20 +118,18 @@
         pair[o].wait_recv()
         up2[o], down2[o] = slab(d_sib, o, depth=d_up), slab(d_sib, o, depth=d_down)
 
-    def slabs_on(o):
+    def slabs_sib_on(o):
         up[o].wait_recv()
-        up3[o] = slab(d_down, o, 1, depth=d_up)
+        up2[o].wait_recv()
+        piece = hs.at[pl.ds(2 * (d_down // 2), 2), o, pl.ds(256, 256)]
+        up3[o] = send(piece, piece, depth=d_up)
         down[o].wait_recv()
-        down3[o] = slab(d_up, o, 0, depth=d_down)
-
-    def slabs_sib_on(o):
-        up2[o].wait_recv()
-        up4[o] = slab(other(d_down), o, 1, depth=d_up)
         down2[o].wait_recv()
-        down4[o] = slab(other(d_up), o, 0, depth=d_down)
+        piece = hs.at[pl.ds(2 * (d_up // 2), 2), o, pl.ds(0, 256)]
+        down3[o] = send(piece, piece, depth=d_down)
 
     def slabs_end(o):
-        for copy in (up3[o], down3[o], up4[o], down4[o]):
+        for copy in (up3[o], down3[o]):
             copy.wait_recv()
 
     z_up = virt(c, j, col=c_up)
@@ -148,7 +146,6 @@
     z_down2 = virt(c_up, j, 0, col=c_down)
     rows_b = virt_rows(c_up)
     slabs_sib(0)
-    slabs_on(0)
     z_up2.wait_recv()
     z_down2.wait_recv()
     rows_c = virt_rows(c_far)
@@ -174,7 +171,6 @@
     slabs_sib_on(0)
     on_c = pass_rows(c_far, rows_c)
     slabs_sib(1)
-    slabs_on(1)
 
     wrow[...] = jnp.zeros_like(wrow)
     for orbital in range(2):
@@ -356,11 +352,13 @@
             red[slot] = total[:, LANES * at : LANES * at + LANES]
         for slot in slots:
             to = rows_of[slot]
+            if slot in (2, 4, 5):
+                links.plan(red.at[slot], tile_land.at[c], recv_sem=mine, row=to, col=r).start()
+        for slot in slots:
+            to = rows_of[slot]
             copy = links.plan(red.at[slot], tile_land.at[c], recv_sem=mine, col=to)
             straight[slot] = to, copy
             pl.when(to != c)(copy.start)
-            if slot in (2, 4, 5):
-                links.plan(red.at[slot], tile_land.at[c], recv_sem=mine, row=to, col=r).start()
 
     straight = {}
 

time: 105 us -> 105 us (level)
  no operation moved by 1% of the time
where the time goes in v11:
time: 105 us
  Pallas kernels  98.5 us (94%)
  other arithmetic  3.38 us (3%)
  local copies, waits for them, and re-layouts  1.99 us (2%)
    pallas_call x1, Pallas kernels, on_device(): pl.pallas_call(gather_kernel, out_shape=jax.ShapeDtypeStruct((RING, 128,...  98.5 us
    convert_element_type x1, other arithmetic, on_device(): return gram.reshape(1024, 1024).astype(F32)  2.61 us

profile of v11, /device:TPU:1, one launch (start us, length us, event | category | flops | bytes accessed | tf_op | source)
XLA Modules:
  0.0 104.5 jit_solution(5630471511015067649)
XLA Ops:
  0.7 0.8 fusion.weight_ref
  1.4 1.0 copy.6.slabs_ref
  2.4 0.0 copy-start
  2.4 1.0 copy-done
  3.4 98.5 %shard_map.55 = bf16[8,128,1024]{2,1,0:T(8,128)(2,1)S(1)} custom-call(bf16[2,500,128]{2,1,0:T(8,128)(2,1)S(1)} %copy.6.slabs_ref, bf16[432,500]{1,0:T(8,128)(2,1)S(1)} %bitcast.5, f32[2,432]{1,0:T(2,128)S(1)} %fusion.weight_ref), custom_call_target="tpu_custom_call" | custom-call | flops 2700000000 | bytes 3000000 | tf_op jit(solution)/shard_map/pallas_call | solution.py:505
  101.9 2.6 %bitcast_convert_fusion = f32[1024,1024]{1,0:T(8,128)} fusion(bf16[8,128,1024]{2,1,0:T(8,128)(2,1)S(1)} %shard_map.55), kind=kLoop, calls=%fused_computation | loop fusion | flops 1048576 | bytes 6291456 | tf_op jit(solution)/shard_map/convert_element_type | solution.py:544
Async XLA Ops:
  2.4 1.0 copy-start

commit v12 on v11

--- a/solution.py
+++ b/solution.py
@@ -331,7 +331,7 @@
             self.own[:, high] = self.own[:, high] + land[3].astype(F32) + land[4].astype(F32)
 
     plane = lax.rem(d, 2)
-    slots_a, slots_b = (5, 7), (0, 2, 4)
+    slots_a, slots_b = (4, 7), (0, 2, 5)
     ring_a = RingSum(a_raw, a_land, a_keep, a_own)
     ring_b = RingSum(b_raw, b_land, b_keep, b_own)
     b_pair = {}
@@ -362,10 +362,10 @@
 
     straight = {}
 
+    y_up[3, 0].wait_recv()
     gram_b(0, "far")
     gram_b(1, "up")
     gram_b(2, "down")
-    y_up[3, 0].wait_recv()
     y_up[4, 1].wait_recv()
     y_down[4, 0].wait_recv()
     ring_a.give("far", terms_of("far", slots_a))

time: 105 us -> 105 us (level)
  no operation moved by 1% of the time
where the time goes in v12:
time: 105 us
  Pallas kernels  98.5 us (94%)
  other arithmetic  3.38 us (3%)
  local copies, waits for them, and re-layouts  1.99 us (2%)
    pallas_call x1, Pallas kernels, on_device(): pl.pallas_call(gather_kernel, out_shape=jax.ShapeDtypeStruct((RING, 128,...  98.5 us
    convert_element_type x1, other arithmetic, on_device(): return gram.reshape(1024, 1024).astype(F32)  2.61 us

profile of v12, /device:TPU:1, one launch (start us, length us, event | category | flops | bytes accessed | tf_op | source)
XLA Modules:
  0.0 104.6 jit_solution(16753695807849742402)
XLA Ops:
  0.7 0.8 fusion.weight_ref
  1.4 1.0 copy.6.slabs_ref
  2.4 0.0 copy-start
  2.4 1.0 copy-done
  3.4 98.5 %shard_map.55 = bf16[8,128,1024]{2,1,0:T(8,128)(2,1)S(1)} custom-call(bf16[2,500,128]{2,1,0:T(8,128)(2,1)S(1)} %copy.6.slabs_ref, bf16[432,500]{1,0:T(8,128)(2,1)S(1)} %bitcast.5, f32[2,432]{1,0:T(2,128)S(1)} %fusion.weight_ref), custom_call_target="tpu_custom_call" | custom-call | flops 2700000000 | bytes 3000000 | tf_op jit(solution)/shard_map/pallas_call | solution.py:505
  101.9 2.6 %bitcast_convert_fusion = f32[1024,1024]{1,0:T(8,128)} fusion(bf16[8,128,1024]{2,1,0:T(8,128)(2,1)S(1)} %shard_map.55), kind=kLoop, calls=%fused_computation | loop fusion | flops 1048576 | bytes 6291456 | tf_op jit(solution)/shard_map/convert_element_type | solution.py:544
Async XLA Ops:
  2.4 1.0 copy-start

commit v13 on v12

--- a/solution.py
+++ b/solution.py
@@ -238,9 +238,9 @@
     panels_out(0)
     slabs_end(1)
 
-    @pl.loop(0, RING)
-    def _(n):
-        couple(n, 1)
+    left = jnp.concatenate([vq[n, quarter] for n in range(RING) for quarter in range(4)], axis=1)
+    right = jnp.concatenate([hs[n, 1] for n in range(RING)], axis=0)
+    acc[1] = jnp.dot(left, right, preferred_element_type=F32)
 
     panels_out(1)
     first_stage = len(links.copies)

time: 105 us -> 106 us (level)
  Pallas kernels: 98.5 us -> 99.8 us
    pallas_call x1, Pallas kernels: 98.5 us -> 99.8 us  [on_device(): pl.pallas_call(gather_kernel, out_shape=jax.ShapeDtypeStruct((RING, 128,...]
where the time goes in v13:
time: 106 us
  Pallas kernels  99.8 us (94%)
  other arithmetic  3.38 us (3%)
  local copies, waits for them, and re-layouts  1.99 us (2%)
    pallas_call x1, Pallas kernels, on_device(): pl.pallas_call(gather_kernel, out_shape=jax.ShapeDtypeStruct((RING, 128,...  99.8 us
    convert_element_type x1, other arithmetic, on_device(): return gram.reshape(1024, 1024).astype(F32)  2.61 us

profile of v13, /device:TPU:1, one launch (start us, length us, event | category | flops | bytes accessed | tf_op | source)
XLA Modules:
  0.0 105.9 jit_solution(11131719919011706423)
XLA Ops:
  0.7 0.8 fusion.weight_ref
  1.4 1.0 copy.6.slabs_ref
  2.4 0.0 copy-start
  2.4 1.0 copy-done
  3.4 99.8 %shard_map.55 = bf16[8,128,1024]{2,1,0:T(8,128)(2,1)S(1)} custom-call(bf16[2,500,128]{2,1,0:T(8,128)(2,1)S(1)} %copy.6.slabs_ref, bf16[432,500]{1,0:T(8,128)(2,1)S(1)} %bitcast.5, f32[2,432]{1,0:T(2,128)S(1)} %fusion.weight_ref), custom_call_target="tpu_custom_call" | custom-call | flops 2700000000 | bytes 3000000 | tf_op jit(solution)/shard_map/pallas_call | solution.py:505
  103.3 2.6 %bitcast_convert_fusion = f32[1024,1024]{1,0:T(8,128)} fusion(bf16[8,128,1024]{2,1,0:T(8,128)(2,1)S(1)} %shard_map.55), kind=kLoop, calls=%fused_computation | loop fusion | flops 1048576 | bytes 6291456 | tf_op jit(solution)/shard_map/convert_element_type | solution.py:544
Async XLA Ops:
  2.4 1.0 copy-start

commit v14 on v9

--- a/solution.py
+++ b/solution.py
@@ -335,7 +335,7 @@
             self.own[:, high] = self.own[:, high] + land[3].astype(F32) + land[4].astype(F32)
 
     plane = lax.rem(d, 2)
-    slots_a, slots_b = (5, 7), (0, 2, 4)
+    slots_a, slots_b = (0, 2, 4), (5, 7)
     ring_a = RingSum(a_raw, a_land, a_keep, a_own)
     ring_b = RingSum(b_raw, b_land, b_keep, b_own)
     b_pair = {}
@@ -356,36 +356,38 @@
             red[slot] = total[:, LANES * at : LANES * at + LANES]
         for slot in slots:
             to = rows_of[slot]
+            if slot in (2, 4, 5):
+                links.plan(red.at[slot], tile_land.at[c], recv_sem=mine, row=to, col=r).start()
+        for slot in slots:
+            to = rows_of[slot]
             copy = links.plan(red.at[slot], tile_land.at[c], recv_sem=mine, col=to)
             straight[slot] = to, copy
             pl.when(to != c)(copy.start)
-            if slot in (2, 4, 5):
-                links.plan(red.at[slot], tile_land.at[c], recv_sem=mine, row=to, col=r).start()
 
     straight = {}
 
-    gram_b(0, "far")
-    gram_b(1, "up")
-    gram_b(2, "down")
+    ring_a.give("far", terms_of("far", slots_a))
+    ring_a.give("down", terms_of("down", slots_a))
+    ring_a.give("own", terms_of("own", slots_a))
     y_up[3, 0].wait_recv()
     y_up[4, 1].wait_recv()
     y_down[4, 0].wait_recv()
-    ring_a.give("far", terms_of("far", slots_a))
-    ring_a.give("down", terms_of("down", slots_a))
-    pair_b(0, "far")
+    gram_b(1, "up")
     ring_a.give("up", terms_of("up", slots_a))
-    gram_b(3, "own")
+    gram_b(0, "far")
     ring_a.pass_on(1)
     ring_a.pass_on(0)
+    gram_b(2, "down")
+    gram_b(3, "own")
+    pair_b(0, "far")
+    pair_b(2, "down")
     pair_b(1, "up")
-    pair_b(2, "down")
-    ring_a.give("own", terms_of("own", slots_a))
-    links.retire(first_stage)
-    ring_b.pass_on(0)
-    ring_b.pass_on(1)
     ring_a.end()
     a_sib[...] = a_own[1 - plane].astype(BF)
     last = send(a_sib, a_last, depth=d_sib)
+    ring_b.pass_on(1)
+    ring_b.pass_on(0)
+    links.retire(first_stage)
     pair_b(3, "own")
     ring_b.end()
     tiles_out(slots_b, b_own[0].astype(BF))
@@ -518,19 +520,19 @@
             pltpu.VMEM((LANES, 512), F32),
             pltpu.VMEM((2, 432, LANES), F32),
             pltpu.VMEM((2, RING, 128, 432), BF),
-            pltpu.VMEM((6, 2, 64, 256), BF),
-            pltpu.VMEM((6, 2, 64, 256), BF),
-            pltpu.VMEM((2, 2, 64, 256), F32),
-            pltpu.VMEM((2, 128, 256), F32),
-            pltpu.VMEM((128, 256), BF),
-            pltpu.VMEM((128, 256), BF),
-            pltpu.VMEM((4, 2, 128, 384), F32),
-            pltpu.VMEM((6, 1, 64, 384), BF),
-            pltpu.VMEM((6, 1, 64, 384), BF),
-            pltpu.VMEM((2, 1, 64, 384), F32),
-            pltpu.VMEM((1, 128, 384), F32),
-            pltpu.VMEM((4, 128, 384), BF),
-            pltpu.VMEM((4, 128, 384), BF),
+            pltpu.VMEM((6, 2, 64, 384), BF),
+            pltpu.VMEM((6, 2, 64, 384), BF),
+            pltpu.VMEM((2, 2, 64, 384), F32),
+            pltpu.VMEM((2, 128, 384), F32),
+            pltpu.VMEM((128, 384), BF),
+            pltpu.VMEM((128, 384), BF),
+            pltpu.VMEM((4, 2, 128, 256), F32),
+            pltpu.VMEM((6, 1, 64, 256), BF),
+            pltpu.VMEM((6, 1, 64, 256), BF),
+            pltpu.VMEM((2, 1, 64, 256), F32),
+            pltpu.VMEM((1, 128, 256), F32),
+            pltpu.VMEM((4, 128, 256), BF),
+            pltpu.VMEM((4, 128, 256), BF),
             pltpu.VMEM((RING, 128, LANES), BF),
             pltpu.VMEM((RING, 128, LANES), BF),
             pltpu.VMEM((RING, RING, 128, LANES), BF),

time: 105 us -> 109 us (1.038)
  Pallas kernels: 98.5 us -> 102 us
    pallas_call x1, Pallas kernels: 98.5 us -> 102 us  [on_device(): pl.pallas_call(gather_kernel, out_shape=jax.ShapeDtypeStruct((RING, 128,...]
where the time goes in v14:
time: 109 us; the launch traced here: 108 us
  Pallas kernels  102 us (94%)
  other arithmetic  3.38 us (3%)
  local copies, waits for them, and re-layouts  1.99 us (2%)
    pallas_call x1, Pallas kernels, on_device(): pl.pallas_call(gather_kernel, out_shape=jax.ShapeDtypeStruct((RING, 128,...  102 us
    convert_element_type x1, other arithmetic, on_device(): return gram.reshape(1024, 1024).astype(F32)  2.61 us

profile of v14, /device:TPU:1, one launch (start us, length us, event | category | flops | bytes accessed | tf_op | source)
XLA Modules:
  0.0 108.5 jit_solution(6590713972873415110)
XLA Ops:
  0.7 0.8 fusion.weight_ref
  1.4 1.0 copy.6.slabs_ref
  2.4 0.0 copy-start
  2.4 1.0 copy-done
  3.4 102.4 %shard_map.55 = bf16[8,128,1024]{2,1,0:T(8,128)(2,1)S(1)} custom-call(bf16[2,500,128]{2,1,0:T(8,128)(2,1)S(1)} %copy.6.slabs_ref, bf16[432,500]{1,0:T(8,128)(2,1)S(1)} %bitcast.5, f32[2,432]{1,0:T(2,128)S(1)} %fusion.weight_ref), custom_call_target="tpu_custom_call" | custom-call | flops 2700000000 | bytes 3000000 | tf_op jit(solution)/shard_map/pallas_call | solution.py:509
  105.9 2.6 %bitcast_convert_fusion = f32[1024,1024]{1,0:T(8,128)} fusion(bf16[8,128,1024]{2,1,0:T(8,128)(2,1)S(1)} %shard_map.55), kind=kLoop, calls=%fused_computation | loop fusion | flops 1048576 | bytes 6291456 | tf_op jit(solution)/shard_map/convert_element_type | solution.py:548
Async XLA Ops:
  2.4 1.0 copy-start
